TPU v7x, 512 devices: a whole 4x4x16 slice. The times are simulated.
512 devices in a mesh: row: 32 (over x, z_hi, core), col: 16 (over y, z_lo).
Axes of the slice: x: 4, y: 4, z: 16 (z_hi: 4, z_lo: 4; z = z_hi * 4 + z_lo), core: 2. Of those that a mesh axis runs over, the one named last changes fastest.
Arguments:
- matrix: bfloat16 [16384, 16384], P('col', 'row'), may hold values from -2 to 2
- block_lists: int32 [16, 32, 16], replicated, may hold values from 0 to 32, as said below
Outputs:
- product: float32 [16384, 16384], P('col', 'row')
Inputs may be any that keep to these rules, and one draw needn't show every extreme that they name: `block_lists`: each list holds distinct positions in ascending order, then 32 in unused entries; some device's list is full, and the block rows near one wall group are denser than the rest.
All inputs are finite; a program needn't handle non-finite values.
Results may differ from a plain program's by a relative error of at most 0.0003.
Values may be sent and summed in bfloat16 or wider, within the bound.
No kernel may reach another device: no remote copies, remote signals or barrier semaphores. Data moves between devices by JAX's collectives and lax.ppermute only.
A program may use at most 64 MiB of HBM per device.

v0:
```python
import jax
import jax.numpy as jnp
from jax import lax
from jax.sharding import PartitionSpec as P

BLOCK = 128


def spread(x, axis, root):
    mine = lax.axis_index(axis) == root
    return lax.psum(jnp.where(mine, x, jnp.zeros_like(x)), axis)


def passed_along(block, axis, distance):
    devices = range(lax.axis_size(axis))
    route = [((i - distance) % len(devices), i) for i in devices]
    return lax.ppermute(block, axis, route)


def body(matrix, block_lists):
    edge_size = BLOCK
    block_rows = matrix.shape[0] // edge_size
    block_cols = matrix.shape[1] // edge_size
    slot_count = block_rows * block_cols
    col_count = lax.axis_size("col")
    col_index = lax.axis_index("col")
    row_index = lax.axis_index("row")
    entries = lax.dynamic_index_in_dim(block_lists, col_index, 0, keepdims=False)
    entries = lax.dynamic_index_in_dim(entries, row_index, 0, keepdims=False)
    own_select = entries[:, None] == jnp.arange(slot_count, dtype=jnp.int32)[None, :]
    occupied = jnp.any(own_select, axis=0).reshape(block_rows, 1, block_cols, 1)
    shaped = matrix.reshape(block_rows, edge_size, block_cols, edge_size)
    masked = jnp.where(occupied, shaped, jnp.zeros_like(shaped)).reshape(matrix.shape)
    half_rows = block_cols * edge_size
    product = jnp.zeros(matrix.shape, jnp.float32)
    lower_slab = masked
    for fox_step in range(2):
        if fox_step == 1:
            lower_slab = passed_along(masked, "col", -1)
        inner_group = (col_index + fox_step) % col_count
        for half_index in range(2):
            arrived = spread(masked, "row", 2 * inner_group + half_index)
            product = product + jnp.dot(
                arrived,
                lower_slab[half_index * half_rows : (half_index + 1) * half_rows],
                preferred_element_type=jnp.float32,
            )
    return product


def solution(mesh):
    return jax.shard_map(
        body,
        mesh=mesh,
        in_specs=(P("col", "row"), P()),
        out_specs=P("col", "row"),
        check_vma=False,
    )
```

profile of v0, /device:TPU:1, one launch (start us, length us, event | category | flops | bytes accessed | tf_op | source)
XLA Modules:
  0.0 435.0 jit_solution(11959932668989347208)
XLA Ops:
  6.5 0.0 copy-start
  6.5 0.0 all-reduce.3.cloned.1.call-start
  6.5 0.9 copy-done
  7.4 0.2 dynamic-slice_reduce_fusion
  7.6 0.1 fusion.12
  7.7 0.1 broadcast_in_dim.19
  7.8 0.3 broadcast_in_dim.20
  8.2 2.5 broadcast_select_fusion
  10.7 1.7 broadcast_select_fusion.2
  12.4 0.0 copy-start.1
  12.4 0.0 all-reduce.3.cloned.1.call-update
  12.4 9.7 %collective-permute-start = (bf16[1024,512]{1,0:T(8,128)(2,1)S(1)}, bf16[1024,512]{1,0:T(8,128)(2,1)}, u32[]{:S(2)}, u32[]{:S(2)}) collective-permute-start(bf16[1024,512]{1,0:T(8,128)(2,1)S(1)} %get-tuple-element.10), channel_id=1, source_target_pairs={{1,0},{2,1},{3,2},{4,3},{5,4},{6,5},{7,6},{8,7},{9,8},{10,9},{11,1... | collective-permute-start | bytes 3145736 | tf_op jit(solution)/shard_map/ppermute | solution.py:17
  22.1 0.0 copy-done.1
  22.1 0.3 reshape.13
  22.4 0.5 broadcast_select_fusion.3
  22.9 0.4 fusion.13
  23.3 396.8 %all-reduce.3.cloned.1.call-done = (bf16[1024,512]{1,0:T(8,128)(2,1)}, bf16[1024,512]{1,0:T(8,128)(2,1)}, bf16[1024,512]{1,0:T(8,128)(2,1)}, bf16[1024,512]{1,0:T(8,128)(2,1)}) async-done(((bf16[1024,512]{1,0:T(8,128)(2,1)}, bf16[1024,512]{1,0:T(8,128)(2,1)}, bf16[1024,512]{1,0:T(8,128)(2,1)}, bf16[1024,512]{1,0:T(8,128)(2,1)}), (bf16[1024,512]{1,0:T(8,128)(2,1)}, bf16[1024,512]{1,0:T(8,128)(2,1)}, ...) | async-done | bytes 4194320 | tf_op jit(solution)/shard_map/psum | solution.py:11
  420.1 0.0 copy-start.4
  420.1 2.0 fusion
  422.1 0.0 copy-start.3
  422.1 0.0 copy-done.4
  422.2 0.7 fusion.3
  422.9 0.0 copy-start.2
  422.9 0.0 collective-permute-done
  422.9 0.5 copy-done.3
  423.4 1.7 fusion.10
  425.1 0.0 copy-done.2
  425.1 3.1 add_add_fusion
Async XLA Ops:
  6.5 0.9 copy-start
  6.5 413.6 %all-reduce.3.cloned.1.call-start = ((), (), s32[]{:S(2)}) async-start(), calls=%async_computation | async-start | bytes 8388608 | tf_op jit(solution)/shard_map/psum | solution.py:11
  12.4 9.7 %copy-start.1 = (bf16[1024,512]{1,0:T(8,128)(2,1)S(1)}, bf16[1024,512]{1,0:T(8,128)(2,1)}, u32[]{:S(2)}) copy-start(bf16[1024,512]{1,0:T(8,128)(2,1)} %param.2) | copy-start | bytes 3145732
  12.4 410.5 %collective-permute-start = (bf16[1024,512]{1,0:T(8,128)(2,1)S(1)}, bf16[1024,512]{1,0:T(8,128)(2,1)}, u32[]{:S(2)}, u32[]{:S(2)}) collective-permute-start(bf16[1024,512]{1,0:T(8,128)(2,1)S(1)} %get-tuple-element.10), channel_id=1, source_target_pairs={{1,0},{2,1},{3,2},{4,3},{5,4},{6,5},{7,6},{8,7},{9,8},{10,9},{11,1... | collective-permute-start | bytes 3145736 | tf_op jit(solution)/shard_map/ppermute | solution.py:17
  420.1 2.0 copy-start.4
  422.1 1.2 copy-start.3
  422.9 2.2 copy-start.2
Sparse Core Ops, SparseCore 0:
  12.5 407.5 all-reduce.2
where the time goes:
time: 439 us; the launch traced here: 435 us
  waiting for transfers between devices  397 us (90%)
  between operations  13.5 us (3%)
  starting transfers between devices  9.67 us (2%)
  matrix products  7.54 us (2%)
  other arithmetic  4.83 us (1%)
    psum x1, waiting for transfers between devices, spread(): return lax.psum(jnp.where(mine, x, jnp.zeros_like(x)), axis)  397 us
    ppermute x1, starting transfers between devices, passed_along(): return lax.ppermute(block, axis, route)  9.67 us
  transfers between devices with their start and end apart: 2, of which 1 were waited for; matrix products, arithmetic and copies ran while one was open for 1% of the time, Pallas kernels for 0%

commit v1 on v0

v1 whole, which is shorter than its diff:
```python
import functools

import jax
import jax.numpy as jnp
from jax import lax
from jax.experimental import pallas as pl
from jax.experimental.pallas import tpu as pltpu
from jax.sharding import PartitionSpec as P

BLOCK = 128
SLOTS = 32
MOST = 16
ROWS, COLS = 1024, 512
BCOLS = COLS // BLOCK
NX, NZ, NC = 4, 4, 2
N_ROW, N_COL = 32, 16
PART = MOST // NX

X_GROUPS = [[x * NZ * NC + i for x in range(NX)] for i in range(NZ * NC)]


def device(x, z, c, g):
    return ((x % NX * NZ + z % NZ) * NC + c) * N_COL + g


def z_moves(moves):
    return [
        (device(x, g + s, c, g), device(x, g + d, c, g))
        for g in range(N_COL)
        for s, d in moves
        for x in range(NX)
        for c in range(NC)
    ]


def pack_kernel(entries, piece, packed):
    for k in range(MOST):
        at = jnp.minimum(entries[k], SLOTS - 1)
        i, j = at // BCOLS, at % BCOLS
        packed[k] = piece[
            pl.ds(pl.multiple_of(i * BLOCK, BLOCK), BLOCK),
            pl.ds(pl.multiple_of(j * BLOCK, BLOCK), BLOCK),
        ]


def pack(matrix, entries):
    return pl.pallas_call(
        pack_kernel,
        out_shape=jax.ShapeDtypeStruct((MOST, BLOCK, BLOCK), matrix.dtype),
        grid_spec=pltpu.PrefetchScalarGridSpec(
            num_scalar_prefetch=1,
            grid=(1,),
            in_specs=[pl.BlockSpec((ROWS, COLS), lambda i, e: (0, 0))],
            out_specs=pl.BlockSpec((MOST, BLOCK, BLOCK), lambda i, e: (0, 0, 0)),
        ),
        compiler_params=pltpu.CompilerParams(vmem_limit_bytes=16 * 2**20),
    )(entries, matrix)


TILE = 256


def product_kernel(lists, left_a, left_b, right_a, right_b, out, left, right):
    core = lists[6, 0]

    @pl.when(pl.program_id(0) == 0)
    def _():
        left[...] = jnp.zeros_like(left)
        right[...] = jnp.zeros_like(right)

        def put_left(part, source, k, column):
            at = lists[column, k]
            i, j = at // BCOLS, at % BCOLS
            left[
                pl.ds(pl.multiple_of(i * BLOCK, BLOCK), BLOCK),
                pl.ds(pl.multiple_of(column * COLS + j * BLOCK, BLOCK), BLOCK),
            ] = source

        for k in range(MOST):
            for step in range(2):
                for ref, c in ((left_a, core), (left_b, 1 - core)):
                    put_left(step, ref[k // PART, step, k % PART], k, step * 2 + c)
        for step, ref in enumerate((right_a, right_b)):
            for k in range(MOST):
                at = lists[4 + step, k]
                i, j = at // BCOLS, at % BCOLS
                right[
                    step,
                    pl.ds(pl.multiple_of(i * BLOCK, BLOCK), BLOCK),
                    pl.ds(pl.multiple_of(j * BLOCK, BLOCK), BLOCK),
                ] = ref[k]

    rows = pl.ds(pl.multiple_of(pl.program_id(0) * TILE, TILE), TILE)
    out[...] = jnp.dot(
        left[rows, : 2 * COLS], right[0, :ROWS], preferred_element_type=jnp.float32
    ) + jnp.dot(
        left[rows, 2 * COLS :], right[1, :ROWS], preferred_element_type=jnp.float32
    )


def multiply(lists, left_a, left_b, right_a, right_b):
    whole = lambda *shape: pl.BlockSpec(shape, lambda i, e: (0,) * len(shape))
    half = (NX, 2, PART, BLOCK, BLOCK)
    piece = (MOST, BLOCK, BLOCK)
    return pl.pallas_call(
        product_kernel,
        out_shape=jax.ShapeDtypeStruct((ROWS, COLS), jnp.float32),
        grid_spec=pltpu.PrefetchScalarGridSpec(
            num_scalar_prefetch=1,
            grid=(ROWS // TILE,),
            in_specs=[whole(*half), whole(*half), whole(*piece), whole(*piece)],
            out_specs=pl.BlockSpec((TILE, COLS), lambda i, e: (i, 0)),
            scratch_shapes=[
                pltpu.VMEM((ROWS + BLOCK, 4 * COLS), jnp.bfloat16),
                pltpu.VMEM((2, ROWS + BLOCK, COLS), jnp.bfloat16),
            ],
        ),
        compiler_params=pltpu.CompilerParams(vmem_limit_bytes=32 * 2**20),
    )(lists, left_a, left_b, right_a, right_b)


def body(matrix, block_lists):
    g, h = lax.axis_index("col"), lax.axis_index("row")
    core, z = h % NC, h // NC % NZ
    at_row = (z - g) % NZ
    flat = block_lists.reshape(N_COL * N_ROW, MOST)
    g_next = (g + 1) % N_COL
    wanted = [g * N_ROW + (2 * g + j) % N_ROW for j in range(4)] + [
        g * N_ROW + h,
        g_next * N_ROW + h,
    ]
    lists = jnp.concatenate(
        [lax.dynamic_slice_in_dim(flat, w, 1, 0) for w in wanted]
        + [jnp.full((2, MOST), core, jnp.int32)]
    )

    own = pack(matrix, lists[4])
    both = ("row", "col")
    below = lax.ppermute(own, "col", [((i + 1) % N_COL, i) for i in range(N_COL)])
    spread = lax.all_to_all(own, "row", 0, 0, axis_index_groups=X_GROUPS, tiled=True)
    spread = spread.reshape(NX, PART, BLOCK, BLOCK)
    source_x = jnp.where(at_row == 1, g_next, g) // NZ
    unit = lax.dynamic_index_in_dim(spread, source_x, 0, keepdims=False)
    other = lax.ppermute(unit, both, z_moves([(0, 1), (1, 0)]))
    first = at_row == 0
    units = jnp.stack([jnp.where(first, unit, other), jnp.where(first, other, unit)])
    outer = lax.ppermute(units, both, z_moves([(0, 3), (1, 2)]))
    units = jnp.where(at_row < 2, units, outer)
    mine = lax.all_to_all(
        jnp.broadcast_to(units[None], (NX, *units.shape)),
        "row", 0, 0, axis_index_groups=X_GROUPS, tiled=True,
    )
    theirs = lax.ppermute(mine, "row", [(i, i ^ 1) for i in range(N_ROW)])
    return multiply(lists, mine, theirs, own, below)


def solution(mesh):
    return jax.shard_map(
        body,
        mesh=mesh,
        in_specs=(P("col", "row"), P()),
        out_specs=P("col", "row"),
        check_vma=False,
    )
```

time: 439 us -> 92.6 us (0.21)
  waiting for transfers between devices: 397 us -> 38.3 us
  starting transfers between devices: 9.67 us -> 27.6 us
  blocking collectives: 0 us -> 15.2 us
  between operations: 13.5 us -> 0.14 us
  Pallas kernels: 0 us -> 8.35 us
  matrix products: 7.54 us -> 0 us
  other arithmetic: 4.83 us -> 0.09 us
    psum x1 -> x0, waiting for transfers between devices: 397 us -> none  [spread(): return lax.psum(jnp.where(mine, x, jnp.zeros_like(x)), axis)]
    ppermute x1 -> x4, waiting for transfers between devices: 0.01 us -> 31.3 us  [the longest x1 22 us: body(): lax.ppermute(own, 'col', [((i + 1) % N_COL, i) for i in range(N_COL)])]
    all_to_all x0 -> x1, blocking collectives: none -> 15.2 us  [body(): lax.all_to_all(jnp.broadcast_to(units[None], (NX, *units.shape)), 'row',...]
    ppermute x1 -> x4, starting transfers between devices: 9.67 us -> 22.8 us  [the longest x1 10.2 us: body(): other = lax.ppermute(unit, both, z_moves([(0, 1), (1, 0)]))]
    pallas_call x0 -> x2, Pallas kernels: none -> 8.35 us  [the longest x1 6.81 us: multiply(): pl.pallas_call(product_kernel, out_shape=jax.ShapeDtypeStruct((ROWS, COLS...]
    dot_general x4 -> x0, matrix products: 7.54 us -> none  [body(): jnp.dot(arrived, lower_slab[half_index * half_rows:(half_index + 1) * hal...]
    all_to_all x0 -> x1, waiting for transfers between devices: none -> 6.93 us  [body(): lax.all_to_all(own, 'row', 0, 0, axis_index_groups=X_GROUPS, tiled=True)]
    all_to_all x0 -> x1, starting transfers between devices: none -> 4.84 us  [body(): lax.all_to_all(own, 'row', 0, 0, axis_index_groups=X_GROUPS, tiled=True)]
  transfers between devices with their start and end apart: 2 -> 5, of which waited for: 1 -> 4; matrix products, arithmetic and copies ran while one was open for 1% -> 0% of each run, Pallas kernels for 0% -> 0%
where the time goes in v1:
time: 92.6 us; the launch traced here: 92.3 us
  waiting for transfers between devices  38.3 us (41%)
  starting transfers between devices  27.6 us (30%)
  blocking collectives  15.2 us (16%)
  Pallas kernels  8.35 us (9%)
  local copies, waits for them, and re-layouts  2.54 us (3%)
    ppermute x1, waiting for transfers between devices, body(): lax.ppermute(own, 'col', [((i + 1) % N_COL, i) for i in range(N_COL)])  22 us
    all_to_all x1, blocking collectives, body(): lax.all_to_all(jnp.broadcast_to(units[None], (NX, *units.shape)), 'row',...  15.2 us
    ppermute x1, starting transfers between devices, body(): other = lax.ppermute(unit, both, z_moves([(0, 1), (1, 0)]))  10.2 us
    ppermute x1, waiting for transfers between devices, body(): outer = lax.ppermute(units, both, z_moves([(0, 3), (1, 2)]))  7.01 us
    all_to_all x1, waiting for transfers between devices, body(): lax.all_to_all(own, 'row', 0, 0, axis_index_groups=X_GROUPS, tiled=True)  6.93 us
    pallas_call x1, Pallas kernels, multiply(): pl.pallas_call(product_kernel, out_shape=jax.ShapeDtypeStruct((ROWS, COLS...  6.81 us
    ppermute x1, starting transfers between devices, body(): lax.ppermute(own, 'col', [((i + 1) % N_COL, i) for i in range(N_COL)])  5.5 us
    ppermute x1, starting transfers between devices, body(): theirs = lax.ppermute(mine, 'row', [(i, i ^ 1) for i in range(N_ROW)])  5.14 us
  transfers between devices with their start and end apart: 5, of which 4 were waited for; matrix products, arithmetic and copies ran while one was open for 0% of the time, Pallas kernels for 0%

profile of v1, /device:TPU:1, one launch (start us, length us, event | category | flops | bytes accessed | tf_op | source)
XLA Modules:
  0.0 92.3 jit_solution(1739593440346741753)
XLA Ops:
  0.0 1.0 %copy.3 = s32[16,32,16]{2,1,0:T(8,128)S(1)} copy(s32[16,32,16]{1,2,0:T(8,128)} %param.3) | data formatting | bytes 65536 | tf_op args[1]
  1.1 0.0 copy-start
  1.1 1.2 %copy-done = bf16[1024,512]{1,0:T(8,128)(2,1)S(1)} copy-done((bf16[1024,512]{1,0:T(8,128)(2,1)S(1)}, bf16[1024,512]{1,0:T(8,128)(2,1)}, u32[]{:S(2)}) %copy-start) | copy-done | bytes 1048600
  2.3 1.5 %shard_map.28.right_a = bf16[16,128,128]{2,1,0:T(8,128)(2,1)} custom-call(s32[16]{0:T(128)S(1)} %bitcast.11, bf16[1024,512]{1,0:T(8,128)(2,1)S(1)} %copy-done), custom_call_target="tpu_custom_call" | custom-call | tf_op jit(solution)/shard_map/pallas_call | solution.py:47
  3.9 4.8 %all-to-all-start = ((bf16[16,128,128]{2,1,0:T(8,128)(2,1)}), bf16[16,128,128]{2,1,0:T(8,128)(2,1)S(1)}, u32[]{:S(2)}, u32[]{:S(2)}) async-start(bf16[16,128,128]{2,1,0:T(8,128)(2,1)} %shard_map.28.right_a), calls=%async_computation | async-start | bytes 1048576 | tf_op jit(solution)/shard_map/all_to_all | solution.py:140
  8.7 6.9 %all-to-all-done = bf16[16,128,128]{2,1,0:T(8,128)(2,1)S(1)} async-done(((bf16[16,128,128]{2,1,0:T(8,128)(2,1)}), bf16[16,128,128]{2,1,0:T(8,128)(2,1)S(1)}, u32[]{:S(2)}, u32[]{:S(2)}) %all-to-all-start) | async-done | bytes 524320 | tf_op jit(solution)/shard_map/all_to_all | solution.py:140
  15.7 10.2 %collective-permute-start = (bf16[4,128,128]{2,1,0:T(8,128)(2,1)S(1)}, bf16[4,128,128]{2,1,0:T(8,128)(2,1)S(1)}, u32[]{:S(2)}, u32[]{:S(2)}) collective-permute-start(bf16[4,128,128]{2,1,0:T(8,128)(2,1)S(1)} %dynamic-slice_bitcast_fusion), channel_id=1, source_target_pairs={{0,32},{16,48},{128,160},{144,176},{256,288},{272,304},{384,416},{... | collective-permute-start | bytes 393224 | tf_op jit(solution)/shard_map/ppermute | solution.py:144
  25.8 2.3 %collective-permute-done = bf16[4,128,128]{2,1,0:T(8,128)(2,1)S(1)} collective-permute-done((bf16[4,128,128]{2,1,0:T(8,128)(2,1)S(1)}, bf16[4,128,128]{2,1,0:T(8,128)(2,1)S(1)}, u32[]{:S(2)}, u32[]{:S(2)}) %collective-permute-start) | collective-permute-done | bytes 131104 | tf_op jit(solution)/shard_map/ppermute | solution.py:144
  28.2 2.0 %collective-permute-start.1 = (bf16[2,4,128,128]{3,2,1,0:T(8,128)(2,1)S(1)}, bf16[2,4,128,128]{3,2,1,0:T(8,128)(2,1)S(1)}, u32[]{:S(2)}, u32[]{:S(2)}) collective-permute-start(bf16[2,4,128,128]{3,2,1,0:T(8,128)(2,1)S(1)} %pad_maximum_fusion), channel_id=1, source_target_pairs={{0,96},{16,112},{128,224},{144,240},{256,352},{272,368},{384,480},... | collective-permute-start | bytes 786440 | tf_op jit(solution)/shard_map/ppermute | solution.py:147
  30.2 7.0 %collective-permute-done.1 = bf16[2,4,128,128]{3,2,1,0:T(8,128)(2,1)S(1)} collective-permute-done((bf16[2,4,128,128]{3,2,1,0:T(8,128)(2,1)S(1)}, bf16[2,4,128,128]{3,2,1,0:T(8,128)(2,1)S(1)}, u32[]{:S(2)}, u32[]{:S(2)}) %collective-permute-start.1) | collective-permute-done | bytes 262176 | tf_op jit(solution)/shard_map/ppermute | solution.py:147
  37.3 0.2 broadcast_in_dim.10
  37.5 15.2 %all_to_all.10.left_a = bf16[4,2,4,128,128]{4,3,2,1,0:T(8,128)(2,1)S(1)} all-to-all(bf16[4,2,4,128,128]{4,3,2,1,0:T(8,128)(2,1)S(1)} %broadcast_in_dim.10), channel_id=1, replica_groups={{0,128,256,384},{16,144,272,400},{32,160,288,416},{48,176,304,432},{64,..., dimensions={0} | all-to-all | bytes 2097152 | tf_op jit(solution)/shard_map/all_to_all | solution.py:149
  52.7 5.1 %collective-permute-start.2 = (bf16[4,2,4,128,128]{4,3,2,1,0:T(8,128)(2,1)S(1)}, bf16[4,2,4,128,128]{4,3,2,1,0:T(8,128)(2,1)S(1)}, u32[]{:S(2)}, u32[]{:S(2)}) collective-permute-start(bf16[4,2,4,128,128]{4,3,2,1,0:T(8,128)(2,1)S(1)} %all_to_all.10.left_a), channel_id=1, source_target_pairs={{0,16},{16,0},{32,48},{48,32},{64,80},{80,64},{96,112},{112,96},{1... | collective-permute-start | bytes 3145736 | tf_op jit(solution)/shard_map/ppermute | solution.py:153
  57.9 5.5 %collective-permute-start.3 = (bf16[16,128,128]{2,1,0:T(8,128)(2,1)}, bf16[16,128,128]{2,1,0:T(8,128)(2,1)S(1)}, u32[]{:S(2)}, u32[]{:S(2)}) collective-permute-start(bf16[16,128,128]{2,1,0:T(8,128)(2,1)} %shard_map.28.right_a), channel_id=1, source_target_pairs={{1,0},{2,1},{3,2},{4,3},{5,4},{6,5},{7,6},{8,7},{9,8},{10,9},{11,1... | collective-permute-start | bytes 1572872 | tf_op jit(solution)/shard_map/ppermute | solution.py:139
  63.5 22.0 %collective-permute-done.3.right_b = bf16[16,128,128]{2,1,0:T(8,128)(2,1)S(1)} collective-permute-done((bf16[16,128,128]{2,1,0:T(8,128)(2,1)}, bf16[16,128,128]{2,1,0:T(8,128)(2,1)S(1)}, u32[]{:S(2)}, u32[]{:S(2)}) %collective-permute-start.3) | collective-permute-done | bytes 524320 | tf_op jit(solution)/shard_map/ppermute | solution.py:139
  85.4 0.0 collective-permute-done.2.left_b
  85.5 6.8 %shard_map.29 = f32[1024,512]{1,0:T(8,128)} custom-call(s32[8,16]{1,0:T(8,128)S(1)} %concatenate.3.lists, bf16[4,2,4,128,128]{4,3,2,1,0:T(8,128)(2,1)S(1)} %all_to_all.10.left_a, bf16[4,2,4,128,128]{4,3,2,1,0:T(8,128)(2,1)S(1)} %collective-permute-done.2.left_b, bf16[16,128,128]{2,1,0:T(8,128)(2,1)} %shard_map.28.right_a, ...), custom_call_target="tpu_custom_call" | custom-call | tf_op jit(solution)/shard_map/pallas_call | solution.py:105
  (7 shorter events, 0.1 us)
Async XLA Ops:
  1.1 1.2 %copy-start = (bf16[1024,512]{1,0:T(8,128)(2,1)S(1)}, bf16[1024,512]{1,0:T(8,128)(2,1)}, u32[]{:S(2)}) copy-start(bf16[1024,512]{1,0:T(8,128)(2,1)} %piece.1) | copy-start | bytes 3145732
  3.9 11.8 %all-to-all-start = ((bf16[16,128,128]{2,1,0:T(8,128)(2,1)}), bf16[16,128,128]{2,1,0:T(8,128)(2,1)S(1)}, u32[]{:S(2)}, u32[]{:S(2)}) async-start(bf16[16,128,128]{2,1,0:T(8,128)(2,1)} %shard_map.28.right_a), calls=%async_computation | async-start | bytes 1048576 | tf_op jit(solution)/shard_map/all_to_all | solution.py:140
  15.7 12.5 %collective-permute-start = (bf16[4,128,128]{2,1,0:T(8,128)(2,1)S(1)}, bf16[4,128,128]{2,1,0:T(8,128)(2,1)S(1)}, u32[]{:S(2)}, u32[]{:S(2)}) collective-permute-start(bf16[4,128,128]{2,1,0:T(8,128)(2,1)S(1)} %dynamic-slice_bitcast_fusion), channel_id=1, source_target_pairs={{0,32},{16,48},{128,160},{144,176},{256,288},{272,304},{384,416},{... | collective-permute-start | bytes 393224 | tf_op jit(solution)/shard_map/ppermute | solution.py:144
  28.2 9.0 %collective-permute-start.1 = (bf16[2,4,128,128]{3,2,1,0:T(8,128)(2,1)S(1)}, bf16[2,4,128,128]{3,2,1,0:T(8,128)(2,1)S(1)}, u32[]{:S(2)}, u32[]{:S(2)}) collective-permute-start(bf16[2,4,128,128]{3,2,1,0:T(8,128)(2,1)S(1)} %pad_maximum_fusion), channel_id=1, source_target_pairs={{0,96},{16,112},{128,224},{144,240},{256,352},{272,368},{384,480},... | collective-permute-start | bytes 786440 | tf_op jit(solution)/shard_map/ppermute | solution.py:147
  52.7 32.7 %collective-permute-start.2 = (bf16[4,2,4,128,128]{4,3,2,1,0:T(8,128)(2,1)S(1)}, bf16[4,2,4,128,128]{4,3,2,1,0:T(8,128)(2,1)S(1)}, u32[]{:S(2)}, u32[]{:S(2)}) collective-permute-start(bf16[4,2,4,128,128]{4,3,2,1,0:T(8,128)(2,1)S(1)} %all_to_all.10.left_a), channel_id=1, source_target_pairs={{0,16},{16,0},{32,48},{48,32},{64,80},{80,64},{96,112},{112,96},{1... | collective-permute-start | bytes 3145736 | tf_op jit(solution)/shard_map/ppermute | solution.py:153
  57.9 27.6 %collective-permute-start.3 = (bf16[16,128,128]{2,1,0:T(8,128)(2,1)}, bf16[16,128,128]{2,1,0:T(8,128)(2,1)S(1)}, u32[]{:S(2)}, u32[]{:S(2)}) collective-permute-start(bf16[16,128,128]{2,1,0:T(8,128)(2,1)} %shard_map.28.right_a), channel_id=1, source_target_pairs={{1,0},{2,1},{3,2},{4,3},{5,4},{6,5},{7,6},{8,7},{9,8},{10,9},{11,1... | collective-permute-start | bytes 1572872 | tf_op jit(solution)/shard_map/ppermute | solution.py:139

commit v2 on v0

v2 whole, which is shorter than its diff:
```python
import jax
import jax.numpy as jnp
from jax import lax
from jax.experimental import pallas as pl
from jax.experimental.pallas import tpu as pltpu
from jax.sharding import PartitionSpec as P

BLOCK = 128
SLOTS = 32
MOST = 16
ROWS, COLS = 1024, 512
BCOLS = COLS // BLOCK
NX, NZ, NC = 4, 4, 2
N_ROW, N_COL = 32, 16
PART = MOST // NX
PIECE = (MOST, BLOCK, BLOCK)
TILE = 256
MIB = 2**20

X_GROUPS = [[x * NZ * NC + i for x in range(NX)] for i in range(NZ * NC)]


def device(x, z, c, g):
    return ((x % NX * NZ + z % NZ) * NC + c) * N_COL + g


def z_moves(moves):
    return [
        (device(x, g + s, c, g), device(x, g + d, c, g))
        for g in range(N_COL)
        for s, d in moves
        for x in range(NX)
        for c in range(NC)
    ]


def place(at):
    return (
        pl.ds(pl.multiple_of(at // BCOLS * BLOCK, BLOCK), BLOCK),
        pl.ds(pl.multiple_of(at % BCOLS * BLOCK, BLOCK), BLOCK),
    )


def pack_kernel(entries, piece, packed):
    for k in range(MOST):
        rows, cols = place(jnp.minimum(entries[k], SLOTS - 1))
        packed[k] = piece[rows, cols]


def pack(matrix, entries):
    return pl.pallas_call(
        pack_kernel,
        out_shape=jax.ShapeDtypeStruct(PIECE, matrix.dtype),
        grid_spec=pltpu.PrefetchScalarGridSpec(
            num_scalar_prefetch=1,
            grid=(1,),
            in_specs=[whole(ROWS, COLS)],
            out_specs=whole(*PIECE),
        ),
        compiler_params=pltpu.CompilerParams(vmem_limit_bytes=16 * MIB),
    )(entries, matrix)


def unpack(lists, which, source, dense):
    dense[...] = jnp.zeros(dense.shape, dense.dtype)
    for k in range(MOST):
        rows, cols = place(lists[which, k])
        dense[rows, cols] = source[k]


def tile_rows():
    return pl.ds(pl.multiple_of(pl.program_id(0) * TILE, TILE), TILE)


def partial_product(left, right, step, c, at):
    inner = pl.ds(pl.multiple_of(c * COLS, COLS), COLS)
    return jnp.dot(left[at], right[step, inner], preferred_element_type=jnp.float32)


def first_kernel(lists, mine, theirs, mine_later, own, below, out, right, left):
    core, flip = lists[6, 0], lists[6, 1]
    parts = ((mine, flip, core), (theirs, flip, 1 - core), (mine_later, 1 - flip, core))

    @pl.when(pl.program_id(0) == 0)
    def _():
        for i, (ref, step, c) in enumerate(parts):
            unpack(lists, step * 2 + c, ref, left.at[i])
        unpack(lists, 4, own, right.at[0])
        unpack(lists, 5, below, right.at[1])

    at = tile_rows()
    total = 0.0
    for i, (_, step, c) in enumerate(parts):
        total += partial_product(left.at[i], right, step, c, at)
    out[...] = total


def second_kernel(lists, theirs, right, partial, out, left):
    core, step = 1 - lists[6, 0], 1 - lists[6, 1]

    @pl.when(pl.program_id(0) == 0)
    def _():
        unpack(lists, step * 2 + core, theirs, left)

    out[...] = partial[...] + partial_product(left, right, step, core, tile_rows())


def whole(*shape):
    return pl.BlockSpec(shape, lambda i, e: (0,) * len(shape))


TILED = pl.BlockSpec((TILE, COLS), lambda i, e: (i, 0))
PRODUCT = jax.ShapeDtypeStruct((ROWS, COLS), jnp.float32)
DENSE = (ROWS + BLOCK, COLS)
RIGHT = jax.ShapeDtypeStruct((2, *DENSE), jnp.bfloat16)


def multiply_first(lists, mine, theirs, mine_later, own, below):
    return pl.pallas_call(
        first_kernel,
        out_shape=(PRODUCT, RIGHT),
        grid_spec=pltpu.PrefetchScalarGridSpec(
            num_scalar_prefetch=1,
            grid=(ROWS // TILE,),
            in_specs=[whole(*PIECE)] * 5,
            out_specs=(TILED, whole(2, *DENSE)),
            scratch_shapes=[pltpu.VMEM((3, *DENSE), jnp.bfloat16)],
        ),
        compiler_params=pltpu.CompilerParams(vmem_limit_bytes=24 * MIB),
        cost_estimate=pl.CostEstimate(flops=2 * ROWS * COLS * 1536, bytes_accessed=8 * MIB, transcendentals=0),
    )(lists, mine, theirs, mine_later, own, below)


def multiply_second(lists, theirs, right, partial):
    return pl.pallas_call(
        second_kernel,
        out_shape=PRODUCT,
        grid_spec=pltpu.PrefetchScalarGridSpec(
            num_scalar_prefetch=1,
            grid=(ROWS // TILE,),
            in_specs=[whole(*PIECE), whole(2, *DENSE), TILED],
            out_specs=TILED,
            scratch_shapes=[pltpu.VMEM(DENSE, jnp.bfloat16)],
        ),
        compiler_params=pltpu.CompilerParams(vmem_limit_bytes=24 * MIB),
    )(lists, theirs, right, partial)


def over_x(unit):
    return lax.all_to_all(
        jnp.broadcast_to(unit[None], (NX, *unit.shape)).reshape(PIECE),
        "row", 0, 0, axis_index_groups=X_GROUPS, tiled=True,
    )


def other_core(pieces):
    return lax.ppermute(pieces, "row", [(i, i ^ 1) for i in range(N_ROW)])


def body(matrix, block_lists):
    g, h = lax.axis_index("col"), lax.axis_index("row")
    core, z = h % NC, h // NC % NZ
    at_row = (z - g) % NZ
    g_next = (g + 1) % N_COL
    flip = ((at_row == 1) | (at_row == 2)).astype(jnp.int32)

    def entries(group, piece):
        return lax.dynamic_slice(block_lists, (group, piece, 0), (1, 1, MOST)).reshape(1, MOST)

    own_list = entries(g, h)
    lists = jnp.concatenate(
        [entries(g, (2 * g + j) % N_ROW) for j in range(4)]
        + [own_list, entries(g_next, h)]
        + [jnp.where(jnp.arange(MOST) == 0, core, flip).astype(jnp.int32)[None]]
    )
    own = pack(matrix, own_list.reshape(MOST))
    both = ("row", "col")
    spread = lax.all_to_all(own, "row", 0, 0, axis_index_groups=X_GROUPS, tiled=True)
    spread = spread.reshape(NX, PART, BLOCK, BLOCK)
    source_x = jnp.where(at_row == 1, g_next, g) // NZ
    unit = lax.dynamic_index_in_dim(spread, source_x, 0, keepdims=False)
    outer = lax.ppermute(unit, both, z_moves([(0, 3), (1, 2)]))
    unit = jnp.where(at_row < 2, unit, outer)
    other = lax.ppermute(unit, both, z_moves([(0, 1), (1, 0), (2, 3), (3, 2)]))
    own_late, unit = lax.optimization_barrier((own, unit))
    below = lax.ppermute(own_late, "col", [((i + 1) % N_COL, i) for i in range(N_COL)])
    mine = over_x(unit)
    theirs = other_core(mine)
    mine_later = over_x(other)
    mine_later, below = lax.optimization_barrier((mine_later, below))
    theirs_later = other_core(mine_later)
    partial, right = multiply_first(lists, mine, theirs, mine_later, own, below)
    return multiply_second(lists, theirs_later, right, partial)


def solution(mesh):
    return jax.shard_map(
        body,
        mesh=mesh,
        in_specs=(P("col", "row"), P()),
        out_specs=P("col", "row"),
        check_vma=False,
    )
```

time: 439 us -> 76.8 us (0.17)
  waiting for transfers between devices: 397 us -> 12.3 us
  starting transfers between devices: 9.67 us -> 49.7 us
  between operations: 13.5 us -> 0.12 us
  Pallas kernels: 0 us -> 9.88 us
  matrix products: 7.54 us -> 0 us
  other arithmetic: 4.83 us -> 0.02 us
    psum x1 -> x0, waiting for transfers between devices: 397 us -> none  [spread(): return lax.psum(jnp.where(mine, x, jnp.zeros_like(x)), axis)]
    ppermute x1 -> x5, starting transfers between devices: 9.67 us -> 37.4 us  [the longest x1 13.8 us: body(): outer = lax.ppermute(unit, both, z_moves([(0, 3), (1, 2)]))]
    all_to_all x0 -> x3, starting transfers between devices: none -> 12.3 us  [the longest x2 7.45 us: over_x(): lax.all_to_all(jnp.broadcast_to(unit[None], (NX, *unit.shape)).reshape(PI...]
    pallas_call x0 -> x3, Pallas kernels: none -> 9.88 us  [the longest x1 5.01 us: multiply_first(): pl.pallas_call(first_kernel, out_shape=(PRODUCT, RIGHT), grid_spec=pltpu....]
    dot_general x4 -> x0, matrix products: 7.54 us -> none  [body(): jnp.dot(arrived, lower_slab[half_index * half_rows:(half_index + 1) * hal...]
    all_to_all x0 -> x3, waiting for transfers between devices: none -> 6.94 us  [the longest x1 6.93 us: body(): lax.all_to_all(own, 'row', 0, 0, axis_index_groups=X_GROUPS, tiled=True)]
    ppermute x1 -> x5, waiting for transfers between devices: 0.01 us -> 5.38 us  [the longest x1 2.84 us: body(): lax.ppermute(own_late, 'col', [((i + 1) % N_COL, i) for i in range(N_COL)])]
    select_n x3 -> x2, other arithmetic: 4.74 us -> 0.02 us  [the longest x1 0.02 us: body(): unit = jnp.where(at_row < 2, unit, outer)]
  transfers between devices with their start and end apart: 2 -> 8, of which waited for: 1 -> 4; matrix products, arithmetic and copies ran while one was open for 1% -> 1% of each run, Pallas kernels for 0% -> 7%
where the time goes in v2:
time: 76.8 us; the launch traced here: 76.2 us
  starting transfers between devices  49.7 us (65%)
  waiting for transfers between devices  12.3 us (16%)
  Pallas kernels  9.88 us (13%)
  local copies, waits for them, and re-layouts  4.19 us (5%)
    ppermute x1, starting transfers between devices, body(): outer = lax.ppermute(unit, both, z_moves([(0, 3), (1, 2)]))  13.8 us
    ppermute x2, starting transfers between devices, other_core(): return lax.ppermute(pieces, 'row', [(i, i ^ 1) for i in range(N_ROW)])  10.9 us
    all_to_all x2, starting transfers between devices, over_x(): lax.all_to_all(jnp.broadcast_to(unit[None], (NX, *unit.shape)).reshape(PI...  7.45 us
    all_to_all x1, waiting for transfers between devices, body(): lax.all_to_all(own, 'row', 0, 0, axis_index_groups=X_GROUPS, tiled=True)  6.93 us
    ppermute x1, starting transfers between devices, body(): lax.ppermute(own_late, 'col', [((i + 1) % N_COL, i) for i in range(N_COL)])  6.56 us
    ppermute x1, starting transfers between devices, body(): other = lax.ppermute(unit, both, z_moves([(0, 1), (1, 0), (2, 3), (3, 2)]))  6.11 us
    pallas_call x1, Pallas kernels, multiply_first(): pl.pallas_call(first_kernel, out_shape=(PRODUCT, RIGHT), grid_spec=pltpu....  5.01 us
    all_to_all x1, starting transfers between devices, body(): lax.all_to_all(own, 'row', 0, 0, axis_index_groups=X_GROUPS, tiled=True)  4.84 us
  transfers between devices with their start and end apart: 8, of which 4 were waited for; matrix products, arithmetic and copies ran while one was open for 1% of the time, Pallas kernels for 7%

profile of v2, /device:TPU:1, one launch (start us, length us, event | category | flops | bytes accessed | tf_op | source)
XLA Modules:
  0.0 76.2 jit_solution(11412742676658025026)
XLA Ops:
  0.0 1.1 %dynamic-slice_reduce_fusion = (s32[16]{0:T(128)S(1)}, s32[16]{0:T(128)S(1)}, s32[16]{0:T(128)S(1)}, s32[16]{0:T(128)S(1)}, s32[16]{0:T(128)S(1)}, /*index=5*/s32[16]{0:T(128)S(1)}) fusion(s32[16,32,16]{1,2,0:T(8,128)} %param.3, s32[]{:T(128)S(6)} %select_n.105, s32[]{:T(128)S(6)} %select_n.103, s32[]{:T(128)S(6)} %select_n.94, s32[]{:T(128)S(6)} %select_n.102, ...), kind=kLoop, calls=%fused_computation.2 | loop fusion | bytes 796 | tf_op jit(solution)/shard_map/dynamic_slice | solution.py:168
  1.1 0.0 copy-start
  1.2 1.2 %copy-done = bf16[1024,512]{1,0:T(8,128)(2,1)S(1)} copy-done((bf16[1024,512]{1,0:T(8,128)(2,1)S(1)}, bf16[1024,512]{1,0:T(8,128)(2,1)}, u32[]{:S(2)}) %copy-start) | copy-done | bytes 1048600
  2.4 1.5 %shard_map.28.own = bf16[16,128,128]{2,1,0:T(8,128)(2,1)} custom-call(s32[16]{0:T(128)S(1)} %get-tuple-element.22.entries, bf16[1024,512]{1,0:T(8,128)(2,1)S(1)} %copy-done), custom_call_target="tpu_custom_call" | custom-call | tf_op jit(solution)/shard_map/pallas_call | solution.py:51
  3.9 4.8 %all-to-all-start = ((bf16[16,128,128]{2,1,0:T(8,128)(2,1)}), bf16[16,128,128]{2,1,0:T(8,128)(2,1)S(1)}, u32[]{:S(2)}, u32[]{:S(2)}) async-start(bf16[16,128,128]{2,1,0:T(8,128)(2,1)} %shard_map.28.own), calls=%async_computation | async-start | bytes 1048576 | tf_op jit(solution)/shard_map/all_to_all | solution.py:178
  8.8 6.9 %all-to-all-done = bf16[16,128,128]{2,1,0:T(8,128)(2,1)S(1)} async-done(((bf16[16,128,128]{2,1,0:T(8,128)(2,1)}), bf16[16,128,128]{2,1,0:T(8,128)(2,1)S(1)}, u32[]{:S(2)}, u32[]{:S(2)}) %all-to-all-start) | async-done | bytes 524320 | tf_op jit(solution)/shard_map/all_to_all | solution.py:178
  15.7 13.8 %collective-permute-start = (bf16[4,128,128]{2,1,0:T(8,128)(2,1)S(1)}, bf16[4,128,128]{2,1,0:T(8,128)(2,1)S(1)}, u32[]{:S(2)}, u32[]{:S(2)}) collective-permute-start(bf16[4,128,128]{2,1,0:T(8,128)(2,1)S(1)} %dynamic-slice_bitcast_fusion), channel_id=1, source_target_pairs={{0,96},{16,112},{128,224},{144,240},{256,352},{272,368},{384,480},... | collective-permute-start | bytes 393224 | tf_op jit(solution)/shard_map/ppermute | solution.py:182
  29.5 1.9 %collective-permute-done = bf16[4,128,128]{2,1,0:T(8,128)(2,1)S(1)} collective-permute-done((bf16[4,128,128]{2,1,0:T(8,128)(2,1)S(1)}, bf16[4,128,128]{2,1,0:T(8,128)(2,1)S(1)}, u32[]{:S(2)}, u32[]{:S(2)}) %collective-permute-start) | collective-permute-done | bytes 131104 | tf_op jit(solution)/shard_map/ppermute | solution.py:182
  31.4 0.9 %broadcast_in_dim.24 = bf16[4,4,128,128]{3,2,1,0:T(8,128)(2,1)} broadcast(bf16[4,128,128]{2,1,0:T(8,128)(2,1)S(1)} %broadcast_select_fusion), dimensions={1,2,3} | broadcast | bytes 655360 | tf_op jit(solution)/shard_map/broadcast_in_dim | solution.py:151
  32.3 3.5 %all-to-all-start.2 = ((bf16[16,128,128]{2,1,0:T(8,128)(2,1)}), bf16[16,128,128]{2,1,0:T(8,128)(2,1)S(1)}, u32[]{:S(2)}, u32[]{:S(2)}) async-start(bf16[16,128,128]{2,1,0:T(8,128)(2,1)} %bitcast.3), calls=%async_computation.2 | async-start | bytes 1048576 | tf_op jit(solution)/shard_map/all_to_all | solution.py:150
  35.8 6.1 %collective-permute-start.1 = (bf16[4,128,128]{2,1,0:T(8,128)(2,1)S(1)}, bf16[4,128,128]{2,1,0:T(8,128)(2,1)S(1)}, u32[]{:S(2)}, u32[]{:S(2)}) collective-permute-start(bf16[4,128,128]{2,1,0:T(8,128)(2,1)S(1)} %broadcast_select_fusion), channel_id=1, source_target_pairs={{0,32},{16,48},{128,160},{144,176},{256,288},{272,304},{384,416},{... | collective-permute-start | bytes 393224 | tf_op jit(solution)/shard_map/ppermute | solution.py:184
  41.9 6.6 %collective-permute-start.2 = (bf16[16,128,128]{2,1,0:T(8,128)(2,1)}, bf16[16,128,128]{2,1,0:T(8,128)(2,1)S(1)}, u32[]{:S(2)}, u32[]{:S(2)}) collective-permute-start(bf16[16,128,128]{2,1,0:T(8,128)(2,1)} %shard_map.28.own), channel_id=1, source_target_pairs={{1,0},{2,1},{3,2},{4,3},{5,4},{6,5},{7,6},{8,7},{9,8},{10,9},{11,1... | collective-permute-start | bytes 1572872 | tf_op jit(solution)/shard_map/ppermute | solution.py:186
  48.5 0.6 collective-permute-done.1
  49.1 0.0 all-to-all-done.2.mine
  49.1 0.9 %broadcast_in_dim.23 = bf16[4,4,128,128]{3,2,1,0:T(8,128)(2,1)} broadcast(bf16[4,128,128]{2,1,0:T(8,128)(2,1)S(1)} %collective-permute-done.1), dimensions={1,2,3} | broadcast | bytes 655360 | tf_op jit(solution)/shard_map/broadcast_in_dim | solution.py:151
  50.0 4.0 %all-to-all-start.1 = ((bf16[16,128,128]{2,1,0:T(8,128)(2,1)}), bf16[16,128,128]{2,1,0:T(8,128)(2,1)S(1)}, u32[]{:S(2)}, u32[]{:S(2)}) async-start(bf16[16,128,128]{2,1,0:T(8,128)(2,1)} %bitcast.2), calls=%async_computation.1 | async-start | bytes 1048576 | tf_op jit(solution)/shard_map/all_to_all | solution.py:150
  54.0 5.7 %collective-permute-start.4 = (bf16[16,128,128]{2,1,0:T(8,128)(2,1)S(1)}, bf16[16,128,128]{2,1,0:T(8,128)(2,1)S(1)}, u32[]{:S(2)}, u32[]{:S(2)}) collective-permute-start(bf16[16,128,128]{2,1,0:T(8,128)(2,1)S(1)} %all-to-all-done.2.mine), channel_id=1, source_target_pairs={{0,16},{16,0},{32,48},{48,32},{64,80},{80,64},{96,112},{112,96},{1... | collective-permute-start | bytes 1572872 | tf_op jit(solution)/shard_map/ppermute | solution.py:157
  59.7 2.8 %collective-permute-done.2.below = bf16[16,128,128]{2,1,0:T(8,128)(2,1)S(1)} collective-permute-done((bf16[16,128,128]{2,1,0:T(8,128)(2,1)}, bf16[16,128,128]{2,1,0:T(8,128)(2,1)S(1)}, u32[]{:S(2)}, u32[]{:S(2)}) %collective-permute-start.2) | collective-permute-done | bytes 524320 | tf_op jit(solution)/shard_map/ppermute | solution.py:186
  62.6 0.0 all-to-all-done.1.mine_later
  62.6 5.2 %collective-permute-start.3 = (bf16[16,128,128]{2,1,0:T(8,128)(2,1)S(1)}, bf16[16,128,128]{2,1,0:T(8,128)(2,1)S(1)}, u32[]{:S(2)}, u32[]{:S(2)}) collective-permute-start(bf16[16,128,128]{2,1,0:T(8,128)(2,1)S(1)} %all-to-all-done.1.mine_later), channel_id=1, source_target_pairs={{0,16},{16,0},{32,48},{48,32},{64,80},{80,64},{96,112},{112,96},{1... | collective-permute-start | bytes 1572872 | tf_op jit(solution)/shard_map/ppermute | solution.py:157
  67.9 0.0 collective-permute-done.4.theirs
  67.9 5.0 %shard_map.29 = (f32[1024,512]{1,0:T(8,128)S(1)}, bf16[2,1152,512]{2,1,0:T(8,128)(2,1)S(1)}) custom-call(s32[7,16]{1,0:T(8,128)S(1)} %concatenate.3.lists, bf16[16,128,128]{2,1,0:T(8,128)(2,1)S(1)} %all-to-all-done.2.mine, bf16[16,128,128]{2,1,0:T(8,128)(2,1)S(1)} %collective-permute-done.4.theirs, bf16[16,128,128]{2,1,0:T(8,128)(2,1)S(1)} %all-to-all-done.1.mine_later, ...), custom_call_target="tpu_custom_call" | custom-call | flops 1610612736 | bytes 8388608 | tf_op jit(solution)/shard_map/pallas_call | solution.py:119
  72.9 0.0 collective-permute-done.3.theirs
  72.9 3.3 %shard_map.30 = f32[1024,512]{1,0:T(8,128)} custom-call(s32[7,16]{1,0:T(8,128)S(1)} %concatenate.3.lists, bf16[16,128,128]{2,1,0:T(8,128)(2,1)S(1)} %collective-permute-done.3.theirs, bf16[2,1152,512]{2,1,0:T(8,128)(2,1)S(1)} %get-tuple-element.15.right, f32[1024,512]{1,0:T(8,128)S(1)} %get-tuple-element.16.partial), custom_call_target="tpu_custom_call" | custom-call | tf_op jit(solution)/shard_map/pallas_call | solution.py:135
  (4 shorter events, 0.1 us)
Async XLA Ops:
  1.1 1.2 %copy-start = (bf16[1024,512]{1,0:T(8,128)(2,1)S(1)}, bf16[1024,512]{1,0:T(8,128)(2,1)}, u32[]{:S(2)}) copy-start(bf16[1024,512]{1,0:T(8,128)(2,1)} %piece.1) | copy-start | bytes 3145732
  3.9 11.8 %all-to-all-start = ((bf16[16,128,128]{2,1,0:T(8,128)(2,1)}), bf16[16,128,128]{2,1,0:T(8,128)(2,1)S(1)}, u32[]{:S(2)}, u32[]{:S(2)}) async-start(bf16[16,128,128]{2,1,0:T(8,128)(2,1)} %shard_map.28.own), calls=%async_computation | async-start | bytes 1048576 | tf_op jit(solution)/shard_map/all_to_all | solution.py:178
  15.7 15.7 %collective-permute-start = (bf16[4,128,128]{2,1,0:T(8,128)(2,1)S(1)}, bf16[4,128,128]{2,1,0:T(8,128)(2,1)S(1)}, u32[]{:S(2)}, u32[]{:S(2)}) collective-permute-start(bf16[4,128,128]{2,1,0:T(8,128)(2,1)S(1)} %dynamic-slice_bitcast_fusion), channel_id=1, source_target_pairs={{0,96},{16,112},{128,224},{144,240},{256,352},{272,368},{384,480},... | collective-permute-start | bytes 393224 | tf_op jit(solution)/shard_map/ppermute | solution.py:182
  32.3 16.8 %all-to-all-start.2 = ((bf16[16,128,128]{2,1,0:T(8,128)(2,1)}), bf16[16,128,128]{2,1,0:T(8,128)(2,1)S(1)}, u32[]{:S(2)}, u32[]{:S(2)}) async-start(bf16[16,128,128]{2,1,0:T(8,128)(2,1)} %bitcast.3), calls=%async_computation.2 | async-start | bytes 1048576 | tf_op jit(solution)/shard_map/all_to_all | solution.py:150
  35.8 13.3 %collective-permute-start.1 = (bf16[4,128,128]{2,1,0:T(8,128)(2,1)S(1)}, bf16[4,128,128]{2,1,0:T(8,128)(2,1)S(1)}, u32[]{:S(2)}, u32[]{:S(2)}) collective-permute-start(bf16[4,128,128]{2,1,0:T(8,128)(2,1)S(1)} %broadcast_select_fusion), channel_id=1, source_target_pairs={{0,32},{16,48},{128,160},{144,176},{256,288},{272,304},{384,416},{... | collective-permute-start | bytes 393224 | tf_op jit(solution)/shard_map/ppermute | solution.py:184
  41.9 20.6 %collective-permute-start.2 = (bf16[16,128,128]{2,1,0:T(8,128)(2,1)}, bf16[16,128,128]{2,1,0:T(8,128)(2,1)S(1)}, u32[]{:S(2)}, u32[]{:S(2)}) collective-permute-start(bf16[16,128,128]{2,1,0:T(8,128)(2,1)} %shard_map.28.own), channel_id=1, source_target_pairs={{1,0},{2,1},{3,2},{4,3},{5,4},{6,5},{7,6},{8,7},{9,8},{10,9},{11,1... | collective-permute-start | bytes 1572872 | tf_op jit(solution)/shard_map/ppermute | solution.py:186
  50.0 12.5 %all-to-all-start.1 = ((bf16[16,128,128]{2,1,0:T(8,128)(2,1)}), bf16[16,128,128]{2,1,0:T(8,128)(2,1)S(1)}, u32[]{:S(2)}, u32[]{:S(2)}) async-start(bf16[16,128,128]{2,1,0:T(8,128)(2,1)} %bitcast.2), calls=%async_computation.1 | async-start | bytes 1048576 | tf_op jit(solution)/shard_map/all_to_all | solution.py:150
  54.0 13.9 %collective-permute-start.4 = (bf16[16,128,128]{2,1,0:T(8,128)(2,1)S(1)}, bf16[16,128,128]{2,1,0:T(8,128)(2,1)S(1)}, u32[]{:S(2)}, u32[]{:S(2)}) collective-permute-start(bf16[16,128,128]{2,1,0:T(8,128)(2,1)S(1)} %all-to-all-done.2.mine), channel_id=1, source_target_pairs={{0,16},{16,0},{32,48},{48,32},{64,80},{80,64},{96,112},{112,96},{1... | collective-permute-start | bytes 1572872 | tf_op jit(solution)/shard_map/ppermute | solution.py:157
  62.6 10.3 %collective-permute-start.3 = (bf16[16,128,128]{2,1,0:T(8,128)(2,1)S(1)}, bf16[16,128,128]{2,1,0:T(8,128)(2,1)S(1)}, u32[]{:S(2)}, u32[]{:S(2)}) collective-permute-start(bf16[16,128,128]{2,1,0:T(8,128)(2,1)S(1)} %all-to-all-done.1.mine_later), channel_id=1, source_target_pairs={{0,16},{16,0},{32,48},{48,32},{64,80},{80,64},{96,112},{112,96},{1... | collective-permute-start | bytes 1572872 | tf_op jit(solution)/shard_map/ppermute | solution.py:157

commit v3 on v2

v3 whole, which is shorter than its diff:
```python
import jax
import jax.numpy as jnp
from jax import lax
from jax.experimental import pallas as pl
from jax.experimental.pallas import tpu as pltpu
from jax.sharding import PartitionSpec as P

BLOCK = 128
SLOTS = 32
MOST = 16
ROWS, COLS = 1024, 512
BCOLS = COLS // BLOCK
NX, NZ, NC = 4, 4, 2
N_ROW, N_COL = 32, 16
PART = MOST // NX
PIECE = (MOST, BLOCK, BLOCK)
TILE = 256
MIB = 2**20
VMEM = pl.BlockSpec(memory_space=pltpu.VMEM)

X_GROUPS = [[x * NZ * NC + i for x in range(NX)] for i in range(NZ * NC)]


def device(x, z, c, g):
    return ((x % NX * NZ + z % NZ) * NC + c) * N_COL + g


def x_moves(j):
    return [
        (device(k // NZ, k % NZ, c, g), device(k // NZ + j, k % NZ, c, g))
        for g in range(N_COL)
        for k in (g, (g + 1) % N_COL)
        for c in range(NC)
    ]


def z_moves(moves):
    return [
        (device(x, g + s, c, g), device(x, g + d, c, g))
        for g in range(N_COL)
        for s, d in moves
        for x in range(NX)
        for c in range(NC)
    ]


def place(at):
    return (
        pl.ds(pl.multiple_of(at // BCOLS * BLOCK, BLOCK), BLOCK),
        pl.ds(pl.multiple_of(at % BCOLS * BLOCK, BLOCK), BLOCK),
    )


def pack_kernel(entries, piece, packed):
    for k in range(MOST):
        source = (k + entries[MOST] * PART) % MOST
        rows, cols = place(jnp.minimum(entries[source], SLOTS - 1))
        packed[k // PART, k % PART] = piece[rows, cols]


def pack_quarters_kernel(entries, piece, *quarters):
    for k in range(MOST):
        source = (k + entries[MOST] * PART) % MOST
        rows, cols = place(jnp.minimum(entries[source], SLOTS - 1))
        quarters[k // PART][k % PART] = piece[rows, cols]


def pack(kernel, matrix, entries, shapes):
    return pl.pallas_call(
        kernel,
        out_shape=[jax.ShapeDtypeStruct(s, matrix.dtype) for s in shapes],
        in_specs=[pl.BlockSpec(memory_space=pltpu.SMEM), VMEM],
        out_specs=[VMEM] * len(shapes),
        compiler_params=pltpu.CompilerParams(vmem_limit_bytes=16 * MIB),
    )(entries, matrix)


def unpack(lists, which, source, dense):
    dense[...] = jnp.zeros(dense.shape, dense.dtype)
    for k in range(MOST):
        rows, cols = place(lists[which, k])
        dense[rows, cols] = source[k]


def inner(c):
    return pl.ds(pl.multiple_of(c * COLS, COLS), COLS)


def dense_left(lists, ref, left, c):
    for unit in range(2):
        step = unit ^ lists[6, 1]
        left[step] = jnp.zeros(left.shape[1:], left.dtype)
        for k in range(MOST):
            rows, cols = place(lists[step * 2 + c, k])
            left[step, rows, cols] = ref[k // PART, unit, k % PART]


def half_product(left, right, c, at):
    return jnp.dot(
        left[0, at], right[0, inner(c)], preferred_element_type=jnp.float32
    ) + jnp.dot(left[1, at], right[1, inner(c)], preferred_element_type=jnp.float32)


def first_kernel(lists, mine, own, below, out, right, left):
    core = lists[6, 0]
    dense_left(lists, mine, left, core)
    unpack(lists, 4, own, right.at[0])
    unpack(lists, 5, below, right.at[1])
    for t in range(0, ROWS, TILE):
        at = pl.ds(t, TILE)
        out[at] = half_product(left, right, core, at)


def second_kernel(lists, theirs, right, partial, out, left, done, sem):
    core = 1 - lists[6, 0]
    dense_left(lists, theirs, left, core)
    copies = []
    for i, t in enumerate(range(0, ROWS, TILE)):
        at = pl.ds(t, TILE)
        done[at] = partial[at] + half_product(left, right, core, at)
        copies.append(pltpu.make_async_copy(done.at[at], out.at[at], sem.at[i]))
        copies[-1].start()
    for copy in copies:
        copy.wait()


PRODUCT = jax.ShapeDtypeStruct((ROWS, COLS), jnp.float32)
DENSE = (ROWS + BLOCK, COLS)
RIGHT = jax.ShapeDtypeStruct((2, *DENSE), jnp.bfloat16)


def call(kernel, lists, operands, out_shape, out_specs, scratch, inner_size):
    return pl.pallas_call(
        kernel,
        out_shape=out_shape,
        in_specs=[pl.BlockSpec(memory_space=pltpu.SMEM)] + [VMEM] * len(operands),
        out_specs=out_specs,
        scratch_shapes=scratch,
        compiler_params=pltpu.CompilerParams(vmem_limit_bytes=8 * MIB),
        cost_estimate=pl.CostEstimate(
            flops=2 * ROWS * COLS * inner_size, bytes_accessed=8 * MIB, transcendentals=0
        ),
    )(lists, *operands)


def multiply_first(lists, *operands):
    scratch = [pltpu.VMEM((2, *DENSE), jnp.bfloat16)]
    return call(first_kernel, lists, operands, (PRODUCT, RIGHT), (VMEM, VMEM), scratch, 2 * COLS)


def multiply_second(lists, *operands):
    scratch = [
        pltpu.VMEM((2, *DENSE), jnp.bfloat16),
        pltpu.VMEM((ROWS, COLS), jnp.float32),
        pltpu.SemaphoreType.DMA((ROWS // TILE,)),
    ]
    anywhere = pl.BlockSpec(memory_space=pl.ANY)
    return call(second_kernel, lists, operands, PRODUCT, anywhere, scratch, 2 * COLS)


def over_x(unit):
    return lax.all_to_all(
        jnp.broadcast_to(unit[None], (NX, *unit.shape)),
        "row", 0, 0, axis_index_groups=X_GROUPS, tiled=True,
    )


def other_core(pieces):
    return lax.ppermute(pieces, "row", [(i, i ^ 1) for i in range(N_ROW)])


def body(matrix, block_lists):
    g, h = lax.axis_index("col"), lax.axis_index("row")
    core, z, x = h % NC, h // NC % NZ, h // NC // NZ
    at_row = (z - g) % NZ
    g_next = (g + 1) % N_COL
    flip = ((at_row == 1) | (at_row == 2)).astype(jnp.int32)

    def entries(group, piece):
        return lax.dynamic_slice(block_lists, (group, piece, 0), (1, 1, MOST)).reshape(1, MOST)

    own_list = entries(g, h)
    lists = jnp.concatenate(
        [entries(g, (2 * g + j) % N_ROW) for j in range(4)]
        + [own_list, entries(g_next, h)]
        + [jnp.where(jnp.arange(MOST) == 0, core, flip).astype(jnp.int32)[None]]
    )
    own_list = own_list.reshape(MOST)
    quarters = pack(
        pack_quarters_kernel, matrix, jnp.append(own_list, x.astype(jnp.int32)), [(PART, BLOCK, BLOCK)] * NX
    )
    own = pack(pack_kernel, matrix, jnp.append(own_list, 0), [(NX, PART, BLOCK, BLOCK)])[0]
    own = own.reshape(PIECE)
    both = ("row", "col")
    source = jnp.where(at_row == 1, g_next, g)
    is_source = (at_row < 2) & (x == source // NZ)
    unit = jnp.where(is_source, quarters[0], jnp.zeros_like(quarters[0]))
    for j in (2, 1, 3):
        unit = unit + lax.ppermute(quarters[j], both, x_moves(j))
    outer = lax.ppermute(unit, both, z_moves([(0, 3), (1, 2)]))
    below = lax.ppermute(own, "col", [((i + 1) % N_COL, i) for i in range(N_COL)])
    unit = jnp.where(at_row < 2, unit, outer)
    other = lax.ppermute(unit, both, z_moves([(0, 1), (1, 0), (2, 3), (3, 2)]))
    mine = over_x(jnp.stack([unit, other]))
    mine, below = lax.optimization_barrier((mine, below))
    theirs = other_core(mine)
    partial, right = multiply_first(lists, mine, own, below)
    return multiply_second(lists, theirs, right, partial)


def solution(mesh):
    return jax.shard_map(
        body,
        mesh=mesh,
        in_specs=(P("col", "row"), P()),
        out_specs=P("col", "row"),
        check_vma=False,
    )
```

time: 76.8 us -> 70.1 us (0.913)
  the two profiles are of different devices: /device:TPU:1 before, /device:TPU:131 now
where the time goes in v3:
time: 70.1 us; the launch traced here: 69.6 us
  waiting for transfers between devices  34.9 us (50%)
  starting transfers between devices  23.6 us (34%)
  Pallas kernels  7.19 us (10%)
  local copies, waits for them, and re-layouts  3.62 us (5%)
    ppermute x1, waiting for transfers between devices, body(): other = lax.ppermute(unit, both, z_moves([(0, 1), (1, 0), (2, 3), (3, 2)]))  13 us
    ppermute x1, waiting for transfers between devices, body(): lax.ppermute(own, 'col', [((i + 1) % N_COL, i) for i in range(N_COL)])  9.63 us
    ppermute x1, starting transfers between devices, body(): lax.ppermute(own, 'col', [((i + 1) % N_COL, i) for i in range(N_COL)])  8.6 us
    ppermute x3, waiting for transfers between devices, body(): unit = unit + lax.ppermute(quarters[j], both, x_moves(j))  7.87 us
    pallas_call x2, Pallas kernels, call(): pl.pallas_call(kernel, out_shape=out_shape, in_specs=[pl.BlockSpec(memory...  5.6 us
    all_to_all x1, starting transfers between devices, over_x(): lax.all_to_all(jnp.broadcast_to(unit[None], (NX, *unit.shape)), 'row', 0,...  4.63 us
    ppermute x1, starting transfers between devices, other_core(): return lax.ppermute(pieces, 'row', [(i, i ^ 1) for i in range(N_ROW)])  4.39 us
    ppermute x1, waiting for transfers between devices, body(): outer = lax.ppermute(unit, both, z_moves([(0, 3), (1, 2)]))  4.38 us
  transfers between devices with their start and end apart: 8, of which 4 were waited for; matrix products, arithmetic and copies ran while one was open for 0% of the time, Pallas kernels for 5%

profile of v3, /device:TPU:131, one launch (start us, length us, event | category | flops | bytes accessed | tf_op | source)
XLA Modules:
  0.0 69.6 jit_solution(1381847755837986806)
XLA Ops:
  0.0 1.1 %dynamic-slice_reduce_fusion = (s32[16]{0:T(128)S(1)}, s32[16]{0:T(128)S(1)}, s32[16]{0:T(128)S(1)}, s32[16]{0:T(128)S(1)}, s32[16]{0:T(128)S(1)}, /*index=5*/s32[16]{0:T(128)S(1)}) fusion(s32[16,32,16]{1,2,0:T(8,128)} %param.3, s32[]{:T(128)S(6)} %select_n.111, s32[]{:T(128)S(6)} %select_n.109, s32[]{:T(128)S(6)} %select_n.100, s32[]{:T(128)S(6)} %select_n.108, ...), kind=kLoop, calls=%fused_computation.3 | loop fusion | bytes 796 | tf_op jit(solution)/shard_map/dynamic_slice | solution.py:180
  1.1 0.1 pad_add_fusion.1
  1.2 0.0 copy-start
  1.2 1.2 %copy-done = bf16[1024,512]{1,0:T(8,128)(2,1)S(1)} copy-done((bf16[1024,512]{1,0:T(8,128)(2,1)S(1)}, bf16[1024,512]{1,0:T(8,128)(2,1)}, u32[]{:S(2)}) %copy-start) | copy-done | bytes 1048600
  2.5 0.8 %shard_map.28 = (bf16[4,128,128]{2,1,0:T(8,128)(2,1)S(1)}, bf16[4,128,128]{2,1,0:T(8,128)(2,1)S(1)}, bf16[4,128,128]{2,1,0:T(8,128)(2,1)S(1)}, bf16[4,128,128]{2,1,0:T(8,128)(2,1)S(1)}) custom-call(s32[17]{0:T(128)S(1)} %get-tuple-element.28.entries, bf16[1024,512]{1,0:T(8,128)(2,1)S(1)} %copy-done), custom_call_target="tpu_custom_call" | custom-call | tf_op jit(solution)/shard_map/pallas_call | solution.py:69
  3.3 0.7 collective-permute-start
  3.9 1.3 %collective-permute-start.1 = (bf16[4,128,128]{2,1,0:T(8,128)(2,1)S(1)}, bf16[4,128,128]{2,1,0:T(8,128)(2,1)S(1)}, u32[]{:S(2)}, u32[]{:S(2)}) collective-permute-start(bf16[4,128,128]{2,1,0:T(8,128)(2,1)S(1)} %get-tuple-element.15), channel_id=1, source_target_pairs={{0,128},{16,144},{32,160},{48,176},{33,161},{49,177},{65,193},{81,... | collective-permute-start | bytes 393224 | tf_op jit(solution)/shard_map/ppermute | solution.py:199
  5.2 0.7 collective-permute-start.2
  6.0 0.0 collective-permute-done
  6.0 7.9 %collective-permute-done.1 = bf16[4,128,128]{2,1,0:T(8,128)(2,1)S(1)} collective-permute-done((bf16[4,128,128]{2,1,0:T(8,128)(2,1)S(1)}, bf16[4,128,128]{2,1,0:T(8,128)(2,1)S(1)}, u32[]{:S(2)}, u32[]{:S(2)}) %collective-permute-start.1) | collective-permute-done | bytes 131104 | tf_op jit(solution)/shard_map/ppermute | solution.py:199
  13.9 0.0 collective-permute-done.2
  13.9 0.0 copy-start.1
  13.9 1.4 %collective-permute-start.3 = (bf16[4,128,128]{2,1,0:T(8,128)(2,1)S(1)}, bf16[4,128,128]{2,1,0:T(8,128)(2,1)S(1)}, u32[]{:S(2)}, u32[]{:S(2)}) collective-permute-start(bf16[4,128,128]{2,1,0:T(8,128)(2,1)S(1)} %add_add_fusion), channel_id=1, source_target_pairs={{0,96},{16,112},{128,224},{144,240},{256,352},{272,368},{384,480},... | collective-permute-start | bytes 393224 | tf_op jit(solution)/shard_map/ppermute | solution.py:200
  15.3 4.4 %collective-permute-done.3 = bf16[4,128,128]{2,1,0:T(8,128)(2,1)S(1)} collective-permute-done((bf16[4,128,128]{2,1,0:T(8,128)(2,1)S(1)}, bf16[4,128,128]{2,1,0:T(8,128)(2,1)S(1)}, u32[]{:S(2)}, u32[]{:S(2)}) %collective-permute-start.3) | collective-permute-done | bytes 131104 | tf_op jit(solution)/shard_map/ppermute | solution.py:200
  19.7 1.9 %collective-permute-start.4 = (bf16[4,128,128]{2,1,0:T(8,128)(2,1)S(1)}, bf16[4,128,128]{2,1,0:T(8,128)(2,1)S(1)}, u32[]{:S(2)}, u32[]{:S(2)}) collective-permute-start(bf16[4,128,128]{2,1,0:T(8,128)(2,1)S(1)} %broadcast_select_fusion), channel_id=1, source_target_pairs={{0,32},{16,48},{128,160},{144,176},{256,288},{272,304},{384,416},{... | collective-permute-start | bytes 393224 | tf_op jit(solution)/shard_map/ppermute | solution.py:203
  21.7 13.0 %collective-permute-done.4 = bf16[4,128,128]{2,1,0:T(8,128)(2,1)S(1)} collective-permute-done((bf16[4,128,128]{2,1,0:T(8,128)(2,1)S(1)}, bf16[4,128,128]{2,1,0:T(8,128)(2,1)S(1)}, u32[]{:S(2)}, u32[]{:S(2)}) %collective-permute-start.4) | collective-permute-done | bytes 131104 | tf_op jit(solution)/shard_map/ppermute | solution.py:203
  34.7 1.2 %broadcast_in_dim.21 = bf16[4,2,4,128,128]{4,3,2,1,0:T(8,128)(2,1)} broadcast(bf16[2,4,128,128]{3,2,1,0:T(8,128)(2,1)S(1)} %pad_maximum_fusion), dimensions={1,2,3,4} | broadcast | bytes 1310720 | tf_op jit(solution)/shard_map/broadcast_in_dim | solution.py:163
  35.9 4.6 %all-to-all-start = ((bf16[4,2,4,128,128]{4,3,2,1,0:T(8,128)(2,1)}), bf16[4,2,4,128,128]{4,3,2,1,0:T(8,128)(2,1)S(1)}, u32[]{:S(2)}, u32[]{:S(2)}) async-start(bf16[4,2,4,128,128]{4,3,2,1,0:T(8,128)(2,1)} %broadcast_in_dim.21), calls=%async_computation | async-start | bytes 2097152 | tf_op jit(solution)/shard_map/all_to_all | solution.py:162
  40.5 0.0 copy-done.1
  40.5 0.8 %shard_map.29 = bf16[4,4,128,128]{3,2,1,0:T(8,128)(2,1)S(1)} custom-call(s32[17]{0:T(128)S(1)} %get-tuple-element.27.entries, bf16[1024,512]{1,0:T(8,128)(2,1)S(1)} %copy-done.1), custom_call_target="tpu_custom_call" | custom-call | tf_op jit(solution)/shard_map/pallas_call | solution.py:69
  41.3 8.6 %collective-permute-start.5 = (bf16[16,128,128]{2,1,0:T(8,128)(2,1)S(1)}, bf16[16,128,128]{2,1,0:T(8,128)(2,1)S(1)}, u32[]{:S(2)}, u32[]{:S(2)}) collective-permute-start(bf16[16,128,128]{2,1,0:T(8,128)(2,1)S(1)} %bitcast.10), channel_id=1, source_target_pairs={{1,0},{2,1},{3,2},{4,3},{5,4},{6,5},{7,6},{8,7},{9,8},{10,9},{11,1... | collective-permute-start | bytes 1572872 | tf_op jit(solution)/shard_map/ppermute | solution.py:201
  49.9 9.6 %collective-permute-done.5.below = bf16[16,128,128]{2,1,0:T(8,128)(2,1)S(1)} collective-permute-done((bf16[16,128,128]{2,1,0:T(8,128)(2,1)S(1)}, bf16[16,128,128]{2,1,0:T(8,128)(2,1)S(1)}, u32[]{:S(2)}, u32[]{:S(2)}) %collective-permute-start.5) | collective-permute-done | bytes 524320 | tf_op jit(solution)/shard_map/ppermute | solution.py:201
  59.6 0.0 all-to-all-done.mine
  59.6 4.4 %collective-permute-start.6 = (bf16[4,2,4,128,128]{4,3,2,1,0:T(8,128)(2,1)S(1)}, bf16[4,2,4,128,128]{4,3,2,1,0:T(8,128)(2,1)S(1)}, u32[]{:S(2)}, u32[]{:S(2)}) collective-permute-start(bf16[4,2,4,128,128]{4,3,2,1,0:T(8,128)(2,1)S(1)} %all-to-all-done.mine), channel_id=1, source_target_pairs={{0,16},{16,0},{32,48},{48,32},{64,80},{80,64},{96,112},{112,96},{1... | collective-permute-start | bytes 3145736 | tf_op jit(solution)/shard_map/ppermute | solution.py:169
  64.0 2.6 %shard_map.30 = (f32[1024,512]{1,0:T(8,128)S(1)}, bf16[2,1152,512]{2,1,0:T(8,128)(2,1)S(1)}) custom-call(s32[7,16]{1,0:T(8,128)S(1)} %concatenate.11.lists, bf16[4,2,4,128,128]{4,3,2,1,0:T(8,128)(2,1)S(1)} %all-to-all-done.mine, bf16[16,128,128]{2,1,0:T(8,128)(2,1)S(1)} %bitcast.11, bf16[16,128,128]{2,1,0:T(8,128)(2,1)S(1)} %collective-permute-done.5.below), custom_call_target="tpu_custom_call" | custom-call | flops 1073741824 | bytes 8388608 | tf_op jit(solution)/shard_map/pallas_call | solution.py:133
  66.6 0.0 collective-permute-done.6.theirs
  66.6 3.0 %shard_map.31 = f32[1024,512]{1,0:T(8,128)} custom-call(s32[7,16]{1,0:T(8,128)S(1)} %concatenate.11.lists, bf16[4,2,4,128,128]{4,3,2,1,0:T(8,128)(2,1)S(1)} %collective-permute-done.6.theirs, bf16[2,1152,512]{2,1,0:T(8,128)(2,1)S(1)} %get-tuple-element.19.right, f32[1024,512]{1,0:T(8,128)S(1)} %get-tuple-element.20.partial), custom_call_target="tpu_custom_call" | custom-call | flops 1073741824 | bytes 8388608 | tf_op jit(solution)/shard_map/pallas_call | solution.py:133
  (5 shorter events, 0.1 us)
Async XLA Ops:
  1.2 1.2 %copy-start = (bf16[1024,512]{1,0:T(8,128)(2,1)S(1)}, bf16[1024,512]{1,0:T(8,128)(2,1)}, u32[]{:S(2)}) copy-start(bf16[1024,512]{1,0:T(8,128)(2,1)} %piece.3) | copy-start | bytes 3145732
  3.3 2.7 %collective-permute-start = (bf16[4,128,128]{2,1,0:T(8,128)(2,1)S(1)}, bf16[4,128,128]{2,1,0:T(8,128)(2,1)S(1)}, u32[]{:S(2)}, u32[]{:S(2)}) collective-permute-start(bf16[4,128,128]{2,1,0:T(8,128)(2,1)S(1)} %get-tuple-element.14), channel_id=1, source_target_pairs={{0,256},{16,272},{32,288},{48,304},{33,289},{49,305},{65,321},{81,... | collective-permute-start | bytes 393224 | tf_op jit(solution)/shard_map/ppermute | solution.py:199
  3.9 9.9 %collective-permute-start.1 = (bf16[4,128,128]{2,1,0:T(8,128)(2,1)S(1)}, bf16[4,128,128]{2,1,0:T(8,128)(2,1)S(1)}, u32[]{:S(2)}, u32[]{:S(2)}) collective-permute-start(bf16[4,128,128]{2,1,0:T(8,128)(2,1)S(1)} %get-tuple-element.15), channel_id=1, source_target_pairs={{0,128},{16,144},{32,160},{48,176},{33,161},{49,177},{65,193},{81,... | collective-permute-start | bytes 393224 | tf_op jit(solution)/shard_map/ppermute | solution.py:199
  5.2 8.6 %collective-permute-start.2 = (bf16[4,128,128]{2,1,0:T(8,128)(2,1)S(1)}, bf16[4,128,128]{2,1,0:T(8,128)(2,1)S(1)}, u32[]{:S(2)}, u32[]{:S(2)}) collective-permute-start(bf16[4,128,128]{2,1,0:T(8,128)(2,1)S(1)} %get-tuple-element.16), channel_id=1, source_target_pairs={{0,384},{16,400},{32,416},{48,432},{33,417},{49,433},{65,449},{81,... | collective-permute-start | bytes 393224 | tf_op jit(solution)/shard_map/ppermute | solution.py:199
  13.9 26.6 %copy-start.1 = (bf16[1024,512]{1,0:T(8,128)(2,1)S(1)}, bf16[1024,512]{1,0:T(8,128)(2,1)}, u32[]{:S(2)}) copy-start(bf16[1024,512]{1,0:T(8,128)(2,1)} %piece.3) | copy-start | bytes 3145732
  13.9 5.8 %collective-permute-start.3 = (bf16[4,128,128]{2,1,0:T(8,128)(2,1)S(1)}, bf16[4,128,128]{2,1,0:T(8,128)(2,1)S(1)}, u32[]{:S(2)}, u32[]{:S(2)}) collective-permute-start(bf16[4,128,128]{2,1,0:T(8,128)(2,1)S(1)} %add_add_fusion), channel_id=1, source_target_pairs={{0,96},{16,112},{128,224},{144,240},{256,352},{272,368},{384,480},... | collective-permute-start | bytes 393224 | tf_op jit(solution)/shard_map/ppermute | solution.py:200
  19.7 14.9 %collective-permute-start.4 = (bf16[4,128,128]{2,1,0:T(8,128)(2,1)S(1)}, bf16[4,128,128]{2,1,0:T(8,128)(2,1)S(1)}, u32[]{:S(2)}, u32[]{:S(2)}) collective-permute-start(bf16[4,128,128]{2,1,0:T(8,128)(2,1)S(1)} %broadcast_select_fusion), channel_id=1, source_target_pairs={{0,32},{16,48},{128,160},{144,176},{256,288},{272,304},{384,416},{... | collective-permute-start | bytes 393224 | tf_op jit(solution)/shard_map/ppermute | solution.py:203
  35.9 23.7 %all-to-all-start = ((bf16[4,2,4,128,128]{4,3,2,1,0:T(8,128)(2,1)}), bf16[4,2,4,128,128]{4,3,2,1,0:T(8,128)(2,1)S(1)}, u32[]{:S(2)}, u32[]{:S(2)}) async-start(bf16[4,2,4,128,128]{4,3,2,1,0:T(8,128)(2,1)} %broadcast_in_dim.21), calls=%async_computation | async-start | bytes 2097152 | tf_op jit(solution)/shard_map/all_to_all | solution.py:162
  41.3 18.2 %collective-permute-start.5 = (bf16[16,128,128]{2,1,0:T(8,128)(2,1)S(1)}, bf16[16,128,128]{2,1,0:T(8,128)(2,1)S(1)}, u32[]{:S(2)}, u32[]{:S(2)}) collective-permute-start(bf16[16,128,128]{2,1,0:T(8,128)(2,1)S(1)} %bitcast.10), channel_id=1, source_target_pairs={{1,0},{2,1},{3,2},{4,3},{5,4},{6,5},{7,6},{8,7},{9,8},{10,9},{11,1... | collective-permute-start | bytes 1572872 | tf_op jit(solution)/shard_map/ppermute | solution.py:201
  59.6 7.0 %collective-permute-start.6 = (bf16[4,2,4,128,128]{4,3,2,1,0:T(8,128)(2,1)S(1)}, bf16[4,2,4,128,128]{4,3,2,1,0:T(8,128)(2,1)S(1)}, u32[]{:S(2)}, u32[]{:S(2)}) collective-permute-start(bf16[4,2,4,128,128]{4,3,2,1,0:T(8,128)(2,1)S(1)} %all-to-all-done.mine), channel_id=1, source_target_pairs={{0,16},{16,0},{32,48},{48,32},{64,80},{80,64},{96,112},{112,96},{1... | collective-permute-start | bytes 3145736 | tf_op jit(solution)/shard_map/ppermute | solution.py:169

commit v4 on v3

--- a/solution.py
+++ b/solution.py
@@ -51,28 +51,45 @@
     )
 
 
-def pack_kernel(entries, piece, packed):
+def pack_kernel(lists, matrix, own, *rest):
+    *quarters, entries, piece, list_sem, sem = rest
+    g, h = lax.axis_index("col"), lax.axis_index("row")
+    x = h // (NZ * NC)
+    fetch = pltpu.make_async_copy(lists.at[g], entries, list_sem)
+    fetch.start()
+    loads = []
+    for i in range(NX):
+        rows = pl.ds(i * TILE, TILE)
+        loads.append(pltpu.make_async_copy(matrix.at[rows], piece.at[rows], sem.at[i]))
+        loads[-1].start()
+    fetch.wait()
+    for load in loads:
+        load.wait()
     for k in range(MOST):
-        source = (k + entries[MOST] * PART) % MOST
-        rows, cols = place(jnp.minimum(entries[source], SLOTS - 1))
-        packed[k // PART, k % PART] = piece[rows, cols]
-
-
-def pack_quarters_kernel(entries, piece, *quarters):
-    for k in range(MOST):
-        source = (k + entries[MOST] * PART) % MOST
-        rows, cols = place(jnp.minimum(entries[source], SLOTS - 1))
-        quarters[k // PART][k % PART] = piece[rows, cols]
-
-
-def pack(kernel, matrix, entries, shapes):
+        rows, cols = place(jnp.minimum(entries[k, h], SLOTS - 1))
+        own[k] = piece[rows, cols]
+    for j, quarter in enumerate(quarters):
+        first = (x + j) % NX * PART
+        for k in range(PART):
+            quarter[k] = own[first + k]
+
+
+def pack(matrix, lists):
+    anywhere = pl.BlockSpec(memory_space=pl.ANY)
+    shapes = [PIECE] + [(PART, BLOCK, BLOCK)] * NX
     return pl.pallas_call(
-        kernel,
+        pack_kernel,
         out_shape=[jax.ShapeDtypeStruct(s, matrix.dtype) for s in shapes],
-        in_specs=[pl.BlockSpec(memory_space=pltpu.SMEM), VMEM],
+        in_specs=[anywhere, anywhere],
         out_specs=[VMEM] * len(shapes),
-        compiler_params=pltpu.CompilerParams(vmem_limit_bytes=16 * MIB),
-    )(entries, matrix)
+        scratch_shapes=[
+            pltpu.SMEM((MOST, N_ROW), jnp.int32),
+            pltpu.VMEM((ROWS, COLS), jnp.bfloat16),
+            pltpu.SemaphoreType.DMA,
+            pltpu.SemaphoreType.DMA((NX,)),
+        ],
+        compiler_params=pltpu.CompilerParams(vmem_limit_bytes=56 * MIB),
+    )(lists, matrix)
 
 
 def unpack(lists, which, source, dense):
@@ -179,24 +196,20 @@
     def entries(group, piece):
         return lax.dynamic_slice(block_lists, (group, piece, 0), (1, 1, MOST)).reshape(1, MOST)
 
-    own_list = entries(g, h)
+    own, *quarters = pack(matrix, jnp.transpose(block_lists, (0, 2, 1)))
+    both = ("row", "col")
+    block_lists, own = lax.optimization_barrier((block_lists, own))
     lists = jnp.concatenate(
         [entries(g, (2 * g + j) % N_ROW) for j in range(4)]
-        + [own_list, entries(g_next, h)]
+        + [entries(g, h), entries(g_next, h)]
         + [jnp.where(jnp.arange(MOST) == 0, core, flip).astype(jnp.int32)[None]]
     )
-    own_list = own_list.reshape(MOST)
-    quarters = pack(
-        pack_quarters_kernel, matrix, jnp.append(own_list, x.astype(jnp.int32)), [(PART, BLOCK, BLOCK)] * NX
-    )
-    own = pack(pack_kernel, matrix, jnp.append(own_list, 0), [(NX, PART, BLOCK, BLOCK)])[0]
-    own = own.reshape(PIECE)
-    both = ("row", "col")
     source = jnp.where(at_row == 1, g_next, g)
     is_source = (at_row < 2) & (x == source // NZ)
     unit = jnp.where(is_source, quarters[0], jnp.zeros_like(quarters[0]))
-    for j in (2, 1, 3):
+    for j in (1, 3, 2):
         unit = unit + lax.ppermute(quarters[j], both, x_moves(j))
+    lists, unit = lax.optimization_barrier((lists, unit))
     outer = lax.ppermute(unit, both, z_moves([(0, 3), (1, 2)]))
     below = lax.ppermute(own, "col", [((i + 1) % N_COL, i) for i in range(N_COL)])
     unit = jnp.where(at_row < 2, unit, outer)

time: 70.1 us -> 69.3 us (0.989)
  waiting for transfers between devices: 34.9 us -> 31.2 us
  starting transfers between devices: 23.6 us -> 26.9 us
  local copies, waits for them, and re-layouts: 3.62 us -> 2.4 us
  Pallas kernels: 7.19 us -> 8 us
    ppermute x3, waiting for transfers between devices: 7.87 us -> 2.47 us  [body(): unit = unit + lax.ppermute(quarters[j], both, x_moves(j))]
    ppermute x1, starting transfers between devices: 1.43 us -> 5.9 us  [body(): outer = lax.ppermute(unit, both, z_moves([(0, 3), (1, 2)]))]
    unnamed x4 -> x2, local copies, waits for them, and re-layouts: 1.24 us -> 0.01 us
    ppermute x1, starting transfers between devices: 8.6 us -> 7.4 us  [body(): lax.ppermute(own, 'col', [((i + 1) % N_COL, i) for i in range(N_COL)])]
    ppermute x1, waiting for transfers between devices: 4.38 us -> 5.55 us  [body(): outer = lax.ppermute(unit, both, z_moves([(0, 3), (1, 2)]))]
    pallas_call x2 -> x1, Pallas kernels: 1.59 us -> 2.38 us  [pack(): pl.pallas_call(pack_kernel, out_shape=[jax.ShapeDtypeStruct(s, matrix.dty...]
  transfers between devices with their start and end apart: 8 -> 8, of which waited for: 4 -> 4; matrix products, arithmetic and copies ran while one was open for 0% -> 2% of each run, Pallas kernels for 5% -> 4%
where the time goes in v4:
time: 69.3 us; the launch traced here: 68.8 us
  waiting for transfers between devices  31.2 us (45%)
  starting transfers between devices  26.9 us (39%)
  Pallas kernels  8 us (12%)
  local copies, waits for them, and re-layouts  2.4 us (3%)
    ppermute x1, waiting for transfers between devices, body(): other = lax.ppermute(unit, both, z_moves([(0, 1), (1, 0), (2, 3), (3, 2)]))  13.3 us
    ppermute x1, waiting for transfers between devices, body(): lax.ppermute(own, 'col', [((i + 1) % N_COL, i) for i in range(N_COL)])  9.91 us
    ppermute x1, starting transfers between devices, body(): lax.ppermute(own, 'col', [((i + 1) % N_COL, i) for i in range(N_COL)])  7.4 us
    ppermute x1, starting transfers between devices, body(): outer = lax.ppermute(unit, both, z_moves([(0, 3), (1, 2)]))  5.9 us
    pallas_call x2, Pallas kernels, call(): pl.pallas_call(kernel, out_shape=out_shape, in_specs=[pl.BlockSpec(memory...  5.62 us
    ppermute x1, waiting for transfers between devices, body(): outer = lax.ppermute(unit, both, z_moves([(0, 3), (1, 2)]))  5.55 us
    all_to_all x1, starting transfers between devices, over_x(): lax.all_to_all(jnp.broadcast_to(unit[None], (NX, *unit.shape)), 'row', 0,...  4.92 us
    ppermute x1, starting transfers between devices, other_core(): return lax.ppermute(pieces, 'row', [(i, i ^ 1) for i in range(N_ROW)])  4.11 us
  transfers between devices with their start and end apart: 8, of which 4 were waited for; matrix products, arithmetic and copies ran while one was open for 2% of the time, Pallas kernels for 4%

profile of v4, /device:TPU:131, one launch (start us, length us, event | category | flops | bytes accessed | tf_op | source)
XLA Modules:
  0.0 68.8 jit_solution(10631940336488831980)
XLA Ops:
  0.0 2.4 %shard_map.28 = (bf16[16,128,128]{2,1,0:T(8,128)(2,1)}, bf16[4,128,128]{2,1,0:T(8,128)(2,1)}, bf16[4,128,128]{2,1,0:T(8,128)(2,1)}, bf16[4,128,128]{2,1,0:T(8,128)(2,1)}, bf16[4,128,128]{2,1,0:T(8,128)(2,1)}) custom-call(s32[16,16,32]{2,1,0:T(8,128)} %bitcast.10, bf16[1024,512]{1,0:T(8,128)(2,1)} %matrix.1), custom_call_target="tpu_custom_call" | custom-call | tf_op jit(solution)/shard_map/pallas_call | solution.py:80
  2.4 1.3 %collective-permute-start = (bf16[4,128,128]{2,1,0:T(8,128)(2,1)}, bf16[4,128,128]{2,1,0:T(8,128)(2,1)S(1)}, u32[]{:S(2)}, u32[]{:S(2)}) collective-permute-start(bf16[4,128,128]{2,1,0:T(8,128)(2,1)} %get-tuple-element.21), channel_id=1, source_target_pairs={{0,128},{16,144},{32,160},{48,176},{33,161},{49,177},{65,193},{81,... | collective-permute-start | bytes 393224 | tf_op jit(solution)/shard_map/ppermute | solution.py:211
  3.7 0.7 collective-permute-start.1
  4.4 0.7 collective-permute-start.2
  5.2 1.2 %dynamic-slice_reduce_fusion = (s32[16]{0:T(128)S(1)}, s32[16]{0:T(128)S(1)}, s32[16]{0:T(128)S(1)}, s32[16]{0:T(128)S(1)}, s32[16]{0:T(128)S(1)}, /*index=5*/s32[16]{0:T(128)S(1)}) fusion(s32[16,32,16]{1,2,0:T(8,128)} %param.3, s32[]{:T(128)S(6)} %select_n.111, s32[]{:T(128)S(6)} %select_n.109, s32[]{:T(128)S(6)} %select_n.100, s32[]{:T(128)S(6)} %select_n.108, ...), kind=kLoop, calls=%fused_computation.3 | loop fusion | bytes 796 | tf_op jit(solution)/shard_map/dynamic_slice | solution.py:197
  6.4 2.5 %collective-permute-done = bf16[4,128,128]{2,1,0:T(8,128)(2,1)S(1)} collective-permute-done((bf16[4,128,128]{2,1,0:T(8,128)(2,1)}, bf16[4,128,128]{2,1,0:T(8,128)(2,1)S(1)}, u32[]{:S(2)}, u32[]{:S(2)}) %collective-permute-start) | collective-permute-done | bytes 131104 | tf_op jit(solution)/shard_map/ppermute | solution.py:211
  8.9 0.0 collective-permute-done.1
  8.9 0.0 collective-permute-done.2
  8.9 0.0 copy-start
  8.9 5.9 %collective-permute-start.3 = (bf16[4,128,128]{2,1,0:T(8,128)(2,1)S(1)}, bf16[4,128,128]{2,1,0:T(8,128)(2,1)S(1)}, u32[]{:S(2)}, u32[]{:S(2)}) collective-permute-start(bf16[4,128,128]{2,1,0:T(8,128)(2,1)S(1)} %add_add_fusion), channel_id=1, source_target_pairs={{0,96},{16,112},{128,224},{144,240},{256,352},{272,368},{384,480},... | collective-permute-start | bytes 393224 | tf_op jit(solution)/shard_map/ppermute | solution.py:213
  14.8 5.5 %collective-permute-done.3 = bf16[4,128,128]{2,1,0:T(8,128)(2,1)S(1)} collective-permute-done((bf16[4,128,128]{2,1,0:T(8,128)(2,1)S(1)}, bf16[4,128,128]{2,1,0:T(8,128)(2,1)S(1)}, u32[]{:S(2)}, u32[]{:S(2)}) %collective-permute-start.3) | collective-permute-done | bytes 131104 | tf_op jit(solution)/shard_map/ppermute | solution.py:213
  20.4 1.9 %collective-permute-start.4 = (bf16[4,128,128]{2,1,0:T(8,128)(2,1)S(1)}, bf16[4,128,128]{2,1,0:T(8,128)(2,1)S(1)}, u32[]{:S(2)}, u32[]{:S(2)}) collective-permute-start(bf16[4,128,128]{2,1,0:T(8,128)(2,1)S(1)} %broadcast_select_fusion), channel_id=1, source_target_pairs={{0,32},{16,48},{128,160},{144,176},{256,288},{272,304},{384,416},{... | collective-permute-start | bytes 393224 | tf_op jit(solution)/shard_map/ppermute | solution.py:216
  22.3 13.3 %collective-permute-done.4 = bf16[4,128,128]{2,1,0:T(8,128)(2,1)S(1)} collective-permute-done((bf16[4,128,128]{2,1,0:T(8,128)(2,1)S(1)}, bf16[4,128,128]{2,1,0:T(8,128)(2,1)S(1)}, u32[]{:S(2)}, u32[]{:S(2)}) %collective-permute-start.4) | collective-permute-done | bytes 131104 | tf_op jit(solution)/shard_map/ppermute | solution.py:216
  35.6 1.2 %broadcast_in_dim.21 = bf16[4,2,4,128,128]{4,3,2,1,0:T(8,128)(2,1)} broadcast(bf16[2,4,128,128]{3,2,1,0:T(8,128)(2,1)S(1)} %pad_maximum_fusion), dimensions={1,2,3,4} | broadcast | bytes 1310720 | tf_op jit(solution)/shard_map/broadcast_in_dim | solution.py:180
  36.8 4.9 %all-to-all-start = ((bf16[4,2,4,128,128]{4,3,2,1,0:T(8,128)(2,1)}), bf16[4,2,4,128,128]{4,3,2,1,0:T(8,128)(2,1)S(1)}, u32[]{:S(2)}, u32[]{:S(2)}) async-start(bf16[4,2,4,128,128]{4,3,2,1,0:T(8,128)(2,1)} %broadcast_in_dim.21), calls=%async_computation | async-start | bytes 2097152 | tf_op jit(solution)/shard_map/all_to_all | solution.py:179
  41.8 0.0 copy-done
  41.8 7.4 %collective-permute-start.5 = (bf16[16,128,128]{2,1,0:T(8,128)(2,1)S(1)}, bf16[16,128,128]{2,1,0:T(8,128)(2,1)S(1)}, u32[]{:S(2)}, u32[]{:S(2)}) collective-permute-start(bf16[16,128,128]{2,1,0:T(8,128)(2,1)S(1)} %copy-done), channel_id=1, source_target_pairs={{1,0},{2,1},{3,2},{4,3},{5,4},{6,5},{7,6},{8,7},{9,8},{10,9},{11,1... | collective-permute-start | bytes 1572872 | tf_op jit(solution)/shard_map/ppermute | solution.py:214
  49.2 9.9 %collective-permute-done.5.below = bf16[16,128,128]{2,1,0:T(8,128)(2,1)S(1)} collective-permute-done((bf16[16,128,128]{2,1,0:T(8,128)(2,1)S(1)}, bf16[16,128,128]{2,1,0:T(8,128)(2,1)S(1)}, u32[]{:S(2)}, u32[]{:S(2)}) %collective-permute-start.5) | collective-permute-done | bytes 524320 | tf_op jit(solution)/shard_map/ppermute | solution.py:214
  59.1 0.0 all-to-all-done.mine
  59.1 4.1 %collective-permute-start.6 = (bf16[4,2,4,128,128]{4,3,2,1,0:T(8,128)(2,1)S(1)}, bf16[4,2,4,128,128]{4,3,2,1,0:T(8,128)(2,1)S(1)}, u32[]{:S(2)}, u32[]{:S(2)}) collective-permute-start(bf16[4,2,4,128,128]{4,3,2,1,0:T(8,128)(2,1)S(1)} %all-to-all-done.mine), channel_id=1, source_target_pairs={{0,16},{16,0},{32,48},{48,32},{64,80},{80,64},{96,112},{112,96},{1... | collective-permute-start | bytes 3145736 | tf_op jit(solution)/shard_map/ppermute | solution.py:186
  63.2 2.6 %shard_map.29 = (f32[1024,512]{1,0:T(8,128)S(1)}, bf16[2,1152,512]{2,1,0:T(8,128)(2,1)S(1)}) custom-call(s32[7,16]{1,0:T(8,128)S(1)} %concatenate.3.lists, bf16[4,2,4,128,128]{4,3,2,1,0:T(8,128)(2,1)S(1)} %all-to-all-done.mine, bf16[16,128,128]{2,1,0:T(8,128)(2,1)S(1)} %copy-done, bf16[16,128,128]{2,1,0:T(8,128)(2,1)S(1)} %collective-permute-done.5.below), custom_call_target="tpu_custom_call" | custom-call | flops 1073741824 | bytes 8388608 | tf_op jit(solution)/shard_map/pallas_call | solution.py:150
  65.8 0.0 collective-permute-done.6.theirs
  65.8 3.0 %shard_map.30 = f32[1024,512]{1,0:T(8,128)} custom-call(s32[7,16]{1,0:T(8,128)S(1)} %concatenate.3.lists, bf16[4,2,4,128,128]{4,3,2,1,0:T(8,128)(2,1)S(1)} %collective-permute-done.6.theirs, bf16[2,1152,512]{2,1,0:T(8,128)(2,1)S(1)} %get-tuple-element.29.right, f32[1024,512]{1,0:T(8,128)S(1)} %get-tuple-element.30.partial), custom_call_target="tpu_custom_call" | custom-call | flops 1073741824 | bytes 8388608 | tf_op jit(solution)/shard_map/pallas_call | solution.py:150
  (5 shorter events, 0.1 us)
Async XLA Ops:
  2.4 6.5 %collective-permute-start = (bf16[4,128,128]{2,1,0:T(8,128)(2,1)}, bf16[4,128,128]{2,1,0:T(8,128)(2,1)S(1)}, u32[]{:S(2)}, u32[]{:S(2)}) collective-permute-start(bf16[4,128,128]{2,1,0:T(8,128)(2,1)} %get-tuple-element.21), channel_id=1, source_target_pairs={{0,128},{16,144},{32,160},{48,176},{33,161},{49,177},{65,193},{81,... | collective-permute-start | bytes 393224 | tf_op jit(solution)/shard_map/ppermute | solution.py:211
  3.7 5.2 %collective-permute-start.1 = (bf16[4,128,128]{2,1,0:T(8,128)(2,1)}, bf16[4,128,128]{2,1,0:T(8,128)(2,1)S(1)}, u32[]{:S(2)}, u32[]{:S(2)}) collective-permute-start(bf16[4,128,128]{2,1,0:T(8,128)(2,1)} %get-tuple-element.22), channel_id=1, source_target_pairs={{0,384},{16,400},{32,416},{48,432},{33,417},{49,433},{65,449},{81,... | collective-permute-start | bytes 393224 | tf_op jit(solution)/shard_map/ppermute | solution.py:211
  4.4 4.5 %collective-permute-start.2 = (bf16[4,128,128]{2,1,0:T(8,128)(2,1)}, bf16[4,128,128]{2,1,0:T(8,128)(2,1)S(1)}, u32[]{:S(2)}, u32[]{:S(2)}) collective-permute-start(bf16[4,128,128]{2,1,0:T(8,128)(2,1)} %get-tuple-element.23), channel_id=1, source_target_pairs={{0,256},{16,272},{32,288},{48,304},{33,289},{49,305},{65,321},{81,... | collective-permute-start | bytes 393224 | tf_op jit(solution)/shard_map/ppermute | solution.py:211
  8.9 32.9 %copy-start = (bf16[16,128,128]{2,1,0:T(8,128)(2,1)S(1)}, bf16[16,128,128]{2,1,0:T(8,128)(2,1)}, u32[]{:S(2)}) copy-start(bf16[16,128,128]{2,1,0:T(8,128)(2,1)} %get-tuple-element.26.own) | copy-start | bytes 1572868
  8.9 11.5 %collective-permute-start.3 = (bf16[4,128,128]{2,1,0:T(8,128)(2,1)S(1)}, bf16[4,128,128]{2,1,0:T(8,128)(2,1)S(1)}, u32[]{:S(2)}, u32[]{:S(2)}) collective-permute-start(bf16[4,128,128]{2,1,0:T(8,128)(2,1)S(1)} %add_add_fusion), channel_id=1, source_target_pairs={{0,96},{16,112},{128,224},{144,240},{256,352},{272,368},{384,480},... | collective-permute-start | bytes 393224 | tf_op jit(solution)/shard_map/ppermute | solution.py:213
  20.4 15.2 %collective-permute-start.4 = (bf16[4,128,128]{2,1,0:T(8,128)(2,1)S(1)}, bf16[4,128,128]{2,1,0:T(8,128)(2,1)S(1)}, u32[]{:S(2)}, u32[]{:S(2)}) collective-permute-start(bf16[4,128,128]{2,1,0:T(8,128)(2,1)S(1)} %broadcast_select_fusion), channel_id=1, source_target_pairs={{0,32},{16,48},{128,160},{144,176},{256,288},{272,304},{384,416},{... | collective-permute-start | bytes 393224 | tf_op jit(solution)/shard_map/ppermute | solution.py:216
  36.8 22.2 %all-to-all-start = ((bf16[4,2,4,128,128]{4,3,2,1,0:T(8,128)(2,1)}), bf16[4,2,4,128,128]{4,3,2,1,0:T(8,128)(2,1)S(1)}, u32[]{:S(2)}, u32[]{:S(2)}) async-start(bf16[4,2,4,128,128]{4,3,2,1,0:T(8,128)(2,1)} %broadcast_in_dim.21), calls=%async_computation | async-start | bytes 2097152 | tf_op jit(solution)/shard_map/all_to_all | solution.py:179
  41.8 17.3 %collective-permute-start.5 = (bf16[16,128,128]{2,1,0:T(8,128)(2,1)S(1)}, bf16[16,128,128]{2,1,0:T(8,128)(2,1)S(1)}, u32[]{:S(2)}, u32[]{:S(2)}) collective-permute-start(bf16[16,128,128]{2,1,0:T(8,128)(2,1)S(1)} %copy-done), channel_id=1, source_target_pairs={{1,0},{2,1},{3,2},{4,3},{5,4},{6,5},{7,6},{8,7},{9,8},{10,9},{11,1... | collective-permute-start | bytes 1572872 | tf_op jit(solution)/shard_map/ppermute | solution.py:214
  59.1 6.7 %collective-permute-start.6 = (bf16[4,2,4,128,128]{4,3,2,1,0:T(8,128)(2,1)S(1)}, bf16[4,2,4,128,128]{4,3,2,1,0:T(8,128)(2,1)S(1)}, u32[]{:S(2)}, u32[]{:S(2)}) collective-permute-start(bf16[4,2,4,128,128]{4,3,2,1,0:T(8,128)(2,1)S(1)} %all-to-all-done.mine), channel_id=1, source_target_pairs={{0,16},{16,0},{32,48},{48,32},{64,80},{80,64},{96,112},{112,96},{1... | collective-permute-start | bytes 3145736 | tf_op jit(solution)/shard_map/ppermute | solution.py:186

commit v5 on v4

--- a/solution.py
+++ b/solution.py
@@ -207,7 +207,7 @@
     source = jnp.where(at_row == 1, g_next, g)
     is_source = (at_row < 2) & (x == source // NZ)
     unit = jnp.where(is_source, quarters[0], jnp.zeros_like(quarters[0]))
-    for j in (1, 3, 2):
+    for j in (1, 2, 3):
         unit = unit + lax.ppermute(quarters[j], both, x_moves(j))
     lists, unit = lax.optimization_barrier((lists, unit))
     outer = lax.ppermute(unit, both, z_moves([(0, 3), (1, 2)]))

time: 69.3 us -> 68.2 us (0.984)
  the two profiles are of different devices: /device:TPU:131 before, /device:TPU:1 now
where the time goes in v5:
time: 68.2 us; the launch traced here: 67.6 us
  starting transfers between devices  35.7 us (52%)
  waiting for transfers between devices  20.2 us (30%)
  Pallas kernels  8 us (12%)
  local copies, waits for them, and re-layouts  2.4 us (4%)
  other arithmetic  0.98 us (1%)
    ppermute x1, waiting for transfers between devices, body(): lax.ppermute(own, 'col', [((i + 1) % N_COL, i) for i in range(N_COL)])  10.9 us
    ppermute x1, starting transfers between devices, body(): other = lax.ppermute(unit, both, z_moves([(0, 1), (1, 0), (2, 3), (3, 2)]))  8.9 us
    ppermute x3, starting transfers between devices, body(): unit = unit + lax.ppermute(quarters[j], both, x_moves(j))  7.45 us
    ppermute x1, waiting for transfers between devices, body(): other = lax.ppermute(unit, both, z_moves([(0, 1), (1, 0), (2, 3), (3, 2)]))  6.36 us
    ppermute x1, starting transfers between devices, body(): outer = lax.ppermute(unit, both, z_moves([(0, 3), (1, 2)]))  6.23 us
    pallas_call x2, Pallas kernels, call(): pl.pallas_call(kernel, out_shape=out_shape, in_specs=[pl.BlockSpec(memory...  5.62 us
    ppermute x1, starting transfers between devices, body(): lax.ppermute(own, 'col', [((i + 1) % N_COL, i) for i in range(N_COL)])  4.98 us
    all_to_all x1, starting transfers between devices, over_x(): lax.all_to_all(jnp.broadcast_to(unit[None], (NX, *unit.shape)), 'row', 0,...  4.33 us
  transfers between devices with their start and end apart: 8, of which 4 were waited for; matrix products, arithmetic and copies ran while one was open for 2% of the time, Pallas kernels for 4%

profile of v5, /device:TPU:1, one launch (start us, length us, event | category | flops | bytes accessed | tf_op | source)
XLA Modules:
  0.0 67.6 jit_solution(17202252698862900096)
XLA Ops:
  0.0 2.4 %shard_map.28 = (bf16[16,128,128]{2,1,0:T(8,128)(2,1)}, bf16[4,128,128]{2,1,0:T(8,128)(2,1)}, bf16[4,128,128]{2,1,0:T(8,128)(2,1)}, bf16[4,128,128]{2,1,0:T(8,128)(2,1)}, bf16[4,128,128]{2,1,0:T(8,128)(2,1)}) custom-call(s32[16,16,32]{2,1,0:T(8,128)} %bitcast.10, bf16[1024,512]{1,0:T(8,128)(2,1)} %matrix.1), custom_call_target="tpu_custom_call" | custom-call | tf_op jit(solution)/shard_map/pallas_call | solution.py:80
  2.4 4.0 %collective-permute-start = (bf16[4,128,128]{2,1,0:T(8,128)(2,1)}, bf16[4,128,128]{2,1,0:T(8,128)(2,1)S(1)}, u32[]{:S(2)}, u32[]{:S(2)}) collective-permute-start(bf16[4,128,128]{2,1,0:T(8,128)(2,1)} %get-tuple-element.21), channel_id=1, source_target_pairs={{0,128},{16,144},{32,160},{48,176},{33,161},{49,177},{65,193},{81,... | collective-permute-start | bytes 393224 | tf_op jit(solution)/shard_map/ppermute | solution.py:211
  6.3 2.2 %collective-permute-start.1 = (bf16[4,128,128]{2,1,0:T(8,128)(2,1)}, bf16[4,128,128]{2,1,0:T(8,128)(2,1)S(1)}, u32[]{:S(2)}, u32[]{:S(2)}) collective-permute-start(bf16[4,128,128]{2,1,0:T(8,128)(2,1)} %get-tuple-element.22), channel_id=1, source_target_pairs={{0,256},{16,272},{32,288},{48,304},{33,289},{49,305},{65,321},{81,... | collective-permute-start | bytes 393224 | tf_op jit(solution)/shard_map/ppermute | solution.py:211
  8.6 1.3 %collective-permute-start.2 = (bf16[4,128,128]{2,1,0:T(8,128)(2,1)}, bf16[4,128,128]{2,1,0:T(8,128)(2,1)S(1)}, u32[]{:S(2)}, u32[]{:S(2)}) collective-permute-start(bf16[4,128,128]{2,1,0:T(8,128)(2,1)} %get-tuple-element.23), channel_id=1, source_target_pairs={{0,384},{16,400},{32,416},{48,432},{33,417},{49,433},{65,449},{81,... | collective-permute-start | bytes 393224 | tf_op jit(solution)/shard_map/ppermute | solution.py:211
  10.0 1.2 %dynamic-slice_reduce_fusion = (s32[16]{0:T(128)S(1)}, s32[16]{0:T(128)S(1)}, s32[16]{0:T(128)S(1)}, s32[16]{0:T(128)S(1)}, s32[16]{0:T(128)S(1)}, /*index=5*/s32[16]{0:T(128)S(1)}) fusion(s32[16,32,16]{1,2,0:T(8,128)} %param.3, s32[]{:T(128)S(6)} %select_n.111, s32[]{:T(128)S(6)} %select_n.109, s32[]{:T(128)S(6)} %select_n.100, s32[]{:T(128)S(6)} %select_n.108, ...), kind=kLoop, calls=%fused_computation.3 | loop fusion | bytes 796 | tf_op jit(solution)/shard_map/dynamic_slice | solution.py:197
  11.2 0.0 collective-permute-done
  11.2 0.0 collective-permute-done.1
  11.2 0.9 %collective-permute-done.2 = bf16[4,128,128]{2,1,0:T(8,128)(2,1)S(1)} collective-permute-done((bf16[4,128,128]{2,1,0:T(8,128)(2,1)}, bf16[4,128,128]{2,1,0:T(8,128)(2,1)S(1)}, u32[]{:S(2)}, u32[]{:S(2)}) %collective-permute-start.2) | collective-permute-done | bytes 131104 | tf_op jit(solution)/shard_map/ppermute | solution.py:211
  12.1 0.9 %add_add_fusion = bf16[4,128,128]{2,1,0:T(8,128)(2,1)S(1)} fusion(bf16[4,128,128]{2,1,0:T(8,128)(2,1)S(1)} %collective-permute-done.2, bf16[4,128,128]{2,1,0:T(8,128)(2,1)S(1)} %collective-permute-done.1, bf16[4,128,128]{2,1,0:T(8,128)(2,1)S(1)} %collective-permute-done, bf16[4,128,128]{2,1,0:T(8,128)(2,1)} %get-tuple-element.20, pred[]{:T(512)S(6)} %and.63), kind=kLoop, calls=%fused_computation.1 | loop fusion | flops 262144 | bytes 655361 | tf_op jit(solution)/shard_map/add | solution.py:211
  13.0 0.0 copy-start
  13.0 6.2 %collective-permute-start.3 = (bf16[4,128,128]{2,1,0:T(8,128)(2,1)S(1)}, bf16[4,128,128]{2,1,0:T(8,128)(2,1)S(1)}, u32[]{:S(2)}, u32[]{:S(2)}) collective-permute-start(bf16[4,128,128]{2,1,0:T(8,128)(2,1)S(1)} %add_add_fusion), channel_id=1, source_target_pairs={{0,96},{16,112},{128,224},{144,240},{256,352},{272,368},{384,480},... | collective-permute-start | bytes 393224 | tf_op jit(solution)/shard_map/ppermute | solution.py:213
  19.3 2.1 %collective-permute-done.3 = bf16[4,128,128]{2,1,0:T(8,128)(2,1)S(1)} collective-permute-done((bf16[4,128,128]{2,1,0:T(8,128)(2,1)S(1)}, bf16[4,128,128]{2,1,0:T(8,128)(2,1)S(1)}, u32[]{:S(2)}, u32[]{:S(2)}) %collective-permute-start.3) | collective-permute-done | bytes 131104 | tf_op jit(solution)/shard_map/ppermute | solution.py:213
  21.4 8.9 %collective-permute-start.4 = (bf16[4,128,128]{2,1,0:T(8,128)(2,1)S(1)}, bf16[4,128,128]{2,1,0:T(8,128)(2,1)S(1)}, u32[]{:S(2)}, u32[]{:S(2)}) collective-permute-start(bf16[4,128,128]{2,1,0:T(8,128)(2,1)S(1)} %broadcast_select_fusion), channel_id=1, source_target_pairs={{0,32},{16,48},{128,160},{144,176},{256,288},{272,304},{384,416},{... | collective-permute-start | bytes 393224 | tf_op jit(solution)/shard_map/ppermute | solution.py:216
  30.3 6.4 %collective-permute-done.4 = bf16[4,128,128]{2,1,0:T(8,128)(2,1)S(1)} collective-permute-done((bf16[4,128,128]{2,1,0:T(8,128)(2,1)S(1)}, bf16[4,128,128]{2,1,0:T(8,128)(2,1)S(1)}, u32[]{:S(2)}, u32[]{:S(2)}) %collective-permute-start.4) | collective-permute-done | bytes 131104 | tf_op jit(solution)/shard_map/ppermute | solution.py:216
  36.7 1.2 %broadcast_in_dim.21 = bf16[4,2,4,128,128]{4,3,2,1,0:T(8,128)(2,1)} broadcast(bf16[2,4,128,128]{3,2,1,0:T(8,128)(2,1)S(1)} %pad_maximum_fusion), dimensions={1,2,3,4} | broadcast | bytes 1310720 | tf_op jit(solution)/shard_map/broadcast_in_dim | solution.py:180
  37.9 4.3 %all-to-all-start = ((bf16[4,2,4,128,128]{4,3,2,1,0:T(8,128)(2,1)}), bf16[4,2,4,128,128]{4,3,2,1,0:T(8,128)(2,1)S(1)}, u32[]{:S(2)}, u32[]{:S(2)}) async-start(bf16[4,2,4,128,128]{4,3,2,1,0:T(8,128)(2,1)} %broadcast_in_dim.21), calls=%async_computation | async-start | bytes 2097152 | tf_op jit(solution)/shard_map/all_to_all | solution.py:179
  42.3 0.0 copy-done
  42.3 5.0 %collective-permute-start.5 = (bf16[16,128,128]{2,1,0:T(8,128)(2,1)S(1)}, bf16[16,128,128]{2,1,0:T(8,128)(2,1)S(1)}, u32[]{:S(2)}, u32[]{:S(2)}) collective-permute-start(bf16[16,128,128]{2,1,0:T(8,128)(2,1)S(1)} %copy-done), channel_id=1, source_target_pairs={{1,0},{2,1},{3,2},{4,3},{5,4},{6,5},{7,6},{8,7},{9,8},{10,9},{11,1... | collective-permute-start | bytes 1572872 | tf_op jit(solution)/shard_map/ppermute | solution.py:214
  47.3 10.9 %collective-permute-done.5.below = bf16[16,128,128]{2,1,0:T(8,128)(2,1)S(1)} collective-permute-done((bf16[16,128,128]{2,1,0:T(8,128)(2,1)S(1)}, bf16[16,128,128]{2,1,0:T(8,128)(2,1)S(1)}, u32[]{:S(2)}, u32[]{:S(2)}) %collective-permute-start.5) | collective-permute-done | bytes 524320 | tf_op jit(solution)/shard_map/ppermute | solution.py:214
  58.1 0.0 all-to-all-done.mine
  58.1 3.8 %collective-permute-start.6 = (bf16[4,2,4,128,128]{4,3,2,1,0:T(8,128)(2,1)S(1)}, bf16[4,2,4,128,128]{4,3,2,1,0:T(8,128)(2,1)S(1)}, u32[]{:S(2)}, u32[]{:S(2)}) collective-permute-start(bf16[4,2,4,128,128]{4,3,2,1,0:T(8,128)(2,1)S(1)} %all-to-all-done.mine), channel_id=1, source_target_pairs={{0,16},{16,0},{32,48},{48,32},{64,80},{80,64},{96,112},{112,96},{1... | collective-permute-start | bytes 3145736 | tf_op jit(solution)/shard_map/ppermute | solution.py:186
  62.0 2.6 %shard_map.29 = (f32[1024,512]{1,0:T(8,128)S(1)}, bf16[2,1152,512]{2,1,0:T(8,128)(2,1)S(1)}) custom-call(s32[7,16]{1,0:T(8,128)S(1)} %concatenate.3.lists, bf16[4,2,4,128,128]{4,3,2,1,0:T(8,128)(2,1)S(1)} %all-to-all-done.mine, bf16[16,128,128]{2,1,0:T(8,128)(2,1)S(1)} %copy-done, bf16[16,128,128]{2,1,0:T(8,128)(2,1)S(1)} %collective-permute-done.5.below), custom_call_target="tpu_custom_call" | custom-call | flops 1073741824 | bytes 8388608 | tf_op jit(solution)/shard_map/pallas_call | solution.py:150
  64.6 0.0 collective-permute-done.6.theirs
  64.6 3.0 %shard_map.30 = f32[1024,512]{1,0:T(8,128)} custom-call(s32[7,16]{1,0:T(8,128)S(1)} %concatenate.3.lists, bf16[4,2,4,128,128]{4,3,2,1,0:T(8,128)(2,1)S(1)} %collective-permute-done.6.theirs, bf16[2,1152,512]{2,1,0:T(8,128)(2,1)S(1)} %get-tuple-element.29.right, f32[1024,512]{1,0:T(8,128)S(1)} %get-tuple-element.30.partial), custom_call_target="tpu_custom_call" | custom-call | flops 1073741824 | bytes 8388608 | tf_op jit(solution)/shard_map/pallas_call | solution.py:150
  (4 shorter events, 0.1 us)
Async XLA Ops:
  2.4 8.8 %collective-permute-start = (bf16[4,128,128]{2,1,0:T(8,128)(2,1)}, bf16[4,128,128]{2,1,0:T(8,128)(2,1)S(1)}, u32[]{:S(2)}, u32[]{:S(2)}) collective-permute-start(bf16[4,128,128]{2,1,0:T(8,128)(2,1)} %get-tuple-element.21), channel_id=1, source_target_pairs={{0,128},{16,144},{32,160},{48,176},{33,161},{49,177},{65,193},{81,... | collective-permute-start | bytes 393224 | tf_op jit(solution)/shard_map/ppermute | solution.py:211
  6.3 4.9 %collective-permute-start.1 = (bf16[4,128,128]{2,1,0:T(8,128)(2,1)}, bf16[4,128,128]{2,1,0:T(8,128)(2,1)S(1)}, u32[]{:S(2)}, u32[]{:S(2)}) collective-permute-start(bf16[4,128,128]{2,1,0:T(8,128)(2,1)} %get-tuple-element.22), channel_id=1, source_target_pairs={{0,256},{16,272},{32,288},{48,304},{33,289},{49,305},{65,321},{81,... | collective-permute-start | bytes 393224 | tf_op jit(solution)/shard_map/ppermute | solution.py:211
  8.6 3.5 %collective-permute-start.2 = (bf16[4,128,128]{2,1,0:T(8,128)(2,1)}, bf16[4,128,128]{2,1,0:T(8,128)(2,1)S(1)}, u32[]{:S(2)}, u32[]{:S(2)}) collective-permute-start(bf16[4,128,128]{2,1,0:T(8,128)(2,1)} %get-tuple-element.23), channel_id=1, source_target_pairs={{0,384},{16,400},{32,416},{48,432},{33,417},{49,433},{65,449},{81,... | collective-permute-start | bytes 393224 | tf_op jit(solution)/shard_map/ppermute | solution.py:211
  13.0 29.2 %copy-start = (bf16[16,128,128]{2,1,0:T(8,128)(2,1)S(1)}, bf16[16,128,128]{2,1,0:T(8,128)(2,1)}, u32[]{:S(2)}) copy-start(bf16[16,128,128]{2,1,0:T(8,128)(2,1)} %get-tuple-element.26.own) | copy-start | bytes 1572868
  13.0 8.4 %collective-permute-start.3 = (bf16[4,128,128]{2,1,0:T(8,128)(2,1)S(1)}, bf16[4,128,128]{2,1,0:T(8,128)(2,1)S(1)}, u32[]{:S(2)}, u32[]{:S(2)}) collective-permute-start(bf16[4,128,128]{2,1,0:T(8,128)(2,1)S(1)} %add_add_fusion), channel_id=1, source_target_pairs={{0,96},{16,112},{128,224},{144,240},{256,352},{272,368},{384,480},... | collective-permute-start | bytes 393224 | tf_op jit(solution)/shard_map/ppermute | solution.py:213
  21.4 15.3 %collective-permute-start.4 = (bf16[4,128,128]{2,1,0:T(8,128)(2,1)S(1)}, bf16[4,128,128]{2,1,0:T(8,128)(2,1)S(1)}, u32[]{:S(2)}, u32[]{:S(2)}) collective-permute-start(bf16[4,128,128]{2,1,0:T(8,128)(2,1)S(1)} %broadcast_select_fusion), channel_id=1, source_target_pairs={{0,32},{16,48},{128,160},{144,176},{256,288},{272,304},{384,416},{... | collective-permute-start | bytes 393224 | tf_op jit(solution)/shard_map/ppermute | solution.py:216
  37.9 20.2 %all-to-all-start = ((bf16[4,2,4,128,128]{4,3,2,1,0:T(8,128)(2,1)}), bf16[4,2,4,128,128]{4,3,2,1,0:T(8,128)(2,1)S(1)}, u32[]{:S(2)}, u32[]{:S(2)}) async-start(bf16[4,2,4,128,128]{4,3,2,1,0:T(8,128)(2,1)} %broadcast_in_dim.21), calls=%async_computation | async-start | bytes 2097152 | tf_op jit(solution)/shard_map/all_to_all | solution.py:179
  42.3 15.9 %collective-permute-start.5 = (bf16[16,128,128]{2,1,0:T(8,128)(2,1)S(1)}, bf16[16,128,128]{2,1,0:T(8,128)(2,1)S(1)}, u32[]{:S(2)}, u32[]{:S(2)}) collective-permute-start(bf16[16,128,128]{2,1,0:T(8,128)(2,1)S(1)} %copy-done), channel_id=1, source_target_pairs={{1,0},{2,1},{3,2},{4,3},{5,4},{6,5},{7,6},{8,7},{9,8},{10,9},{11,1... | collective-permute-start | bytes 1572872 | tf_op jit(solution)/shard_map/ppermute | solution.py:214
  58.1 6.4 %collective-permute-start.6 = (bf16[4,2,4,128,128]{4,3,2,1,0:T(8,128)(2,1)S(1)}, bf16[4,2,4,128,128]{4,3,2,1,0:T(8,128)(2,1)S(1)}, u32[]{:S(2)}, u32[]{:S(2)}) collective-permute-start(bf16[4,2,4,128,128]{4,3,2,1,0:T(8,128)(2,1)S(1)} %all-to-all-done.mine), channel_id=1, source_target_pairs={{0,16},{16,0},{32,48},{48,32},{64,80},{80,64},{96,112},{112,96},{1... | collective-permute-start | bytes 3145736 | tf_op jit(solution)/shard_map/ppermute | solution.py:186
